TPU v7x, 128 devices: a whole 4x4x4 slice. The times are simulated.
128 devices in a mesh: fsdp: 4 (over z_hi, core), blk: 32 (over y, z_lo, x).
Axes of the slice: x: 4, y: 4, z: 4 (z_hi: 2, z_lo: 2; z = z_hi * 2 + z_lo), core: 2. Of those that a mesh axis runs over, the one named last changes fastest.
Arguments:
- query_nope: bfloat16 [4, 4096, 1024], P('fsdp', 'blk'), may hold values from -6 to 6
- query_rope: bfloat16 [4, 4096, 512], P('fsdp', 'blk'), may hold values from -500 to 500
- latent: bfloat16 [4, 4096, 576], P('fsdp', 'blk'), may hold values from -5 to 5
- grad_out: bfloat16 [4, 4096, 1024], P('fsdp', 'blk'), may hold values from -6 to 6
- w_up: bfloat16 [512, 2048], P('fsdp'), may hold values from -0.5 to 0.5
- block_order: int32 [32, 2], replicated, may hold values from 0 to 63, as said below
Outputs:
- grad_query_nope: bfloat16 [4, 4096, 1024], P('fsdp', 'blk')
- grad_query_rope: bfloat16 [4, 4096, 512], P('fsdp', 'blk')
- grad_latent: bfloat16 [4, 4096, 576], P('fsdp', 'blk')
- grad_up: float32 [512, 2048], P(('fsdp', 'blk'))
Inputs may be any that keep to these rules, and one draw needn't show every extreme that they name: block_order[i, 1] = 63 - block_order[i, 0] and block_order[i, 0] < 32; every block 0 to 63 is held by exactly one device.
All inputs are finite; a program needn't handle non-finite values.
Results may differ from a plain program's by a relative error of at most 0.013.
Values may be sent and summed in bfloat16 or wider, within the bound.
A program may use at most 128 MiB of HBM per device.

v0:
```python
import math

import jax
import jax.numpy as jnp
from jax import lax
from jax.sharding import PartitionSpec as P

HEADS = 8
NOPE_DIM = 128
ROPE_DIM = 64
VALUE_DIM = 128
LATENT = 512


NEG_FILL = -1e30


def from_behind(block, axis, distance):
    devices = range(lax.axis_size(axis))
    route = [((i - distance) % len(devices), i) for i in devices]
    return lax.ppermute(block, axis, route)


def half_rows(array, which, half):
    return lax.dynamic_slice_in_dim(array, which * half, half, 0)


def pick_half(stacked, which):
    return lax.dynamic_index_in_dim(stacked, which, 0, keepdims=False)


def put_half(stacked, value, which):
    return lax.dynamic_update_index_in_dim(stacked, value, which, 0)


def circulate(held):
    return from_behind(held, "blk", 1)


def pass_terms(terms):
    return from_behind(terms, "blk", 1)


def masked_scores(query_rows, query_pos, key_rows, key_pos):
    scores = jnp.einsum("thk,uk->htu", query_rows, key_rows, preferred_element_type=jnp.float32)
    scores = scores * (1.0 / math.sqrt(NOPE_DIM + ROPE_DIM))
    allowed = key_pos[None, None, :] <= query_pos[None, :, None]
    return (jnp.where(allowed, scores, NEG_FILL), allowed)


def forward_visit(stats, context, held, held_pos, query_half, key_half):
    query_stack, grad_stack, pos_stack = context
    half = held.shape[0] // 2
    peak, total, weighted = stats
    query_rows = pick_half(query_stack, query_half)
    grad_rows = pick_half(grad_stack, query_half)
    key_rows = half_rows(held, key_half, half)
    scores, allowed = masked_scores(
        query_rows, pick_half(pos_stack, query_half), key_rows, half_rows(held_pos, key_half, half)
    )
    old_peak = pick_half(peak, query_half)
    new_peak = jnp.maximum(old_peak, jnp.max(scores, axis=-1))
    weights = jnp.where(allowed, jnp.exp(scores - new_peak[:, :, None]), 0.0)
    grad_probs = jnp.einsum(
        "thj,uj->htu", grad_rows, key_rows[:, :LATENT], preferred_element_type=jnp.float32
    )
    factor = jnp.exp(old_peak - new_peak)
    total = put_half(
        total, pick_half(total, query_half) * factor + jnp.sum(weights, axis=-1), query_half
    )
    weighted = put_half(
        weighted,
        pick_half(weighted, query_half) * factor + jnp.sum(weights * grad_probs, axis=-1),
        query_half,
    )
    peak = put_half(peak, new_peak, query_half)
    return (peak, total, weighted)


def backward_visit(carry, context, held, held_pos, key_base, query_half, key_half):
    query_stack, grad_stack, pos_stack, norm_log, centre = context
    grad_query, out_latent, key_terms = carry
    half = held.shape[0] // 2
    scale = 1.0 / math.sqrt(NOPE_DIM + ROPE_DIM)
    query_rows = pick_half(query_stack, query_half)
    grad_rows = pick_half(grad_stack, query_half)
    key_rows = half_rows(held, key_half, half)
    scores, allowed = masked_scores(
        query_rows, pick_half(pos_stack, query_half), key_rows, half_rows(held_pos, key_half, half)
    )
    probs = jnp.where(allowed, jnp.exp(scores - pick_half(norm_log, query_half)[:, :, None]), 0.0)
    grad_probs = jnp.einsum(
        "thj,uj->htu", grad_rows, key_rows[:, :LATENT], preferred_element_type=jnp.float32
    )
    grad_scores = probs * (grad_probs - pick_half(centre, query_half)[:, :, None])
    probs_low = probs.astype(jnp.bfloat16)
    grad_low = grad_scores.astype(jnp.bfloat16)
    add_out = jnp.einsum(
        "htu,uj->thj", probs_low, key_rows[:, :LATENT], preferred_element_type=jnp.float32
    )
    add_query = (
        jnp.einsum("htu,uk->thk", grad_low, key_rows, preferred_element_type=jnp.float32) * scale
    )
    term = (
        jnp.einsum("htu,thk->uk", grad_low, query_rows, preferred_element_type=jnp.float32) * scale
    )
    value_term = jnp.einsum("htu,thj->uj", probs_low, grad_rows, preferred_element_type=jnp.float32)
    term = term + jnp.pad(value_term, ((0, 0), (0, ROPE_DIM)))
    grad_query = put_half(grad_query, pick_half(grad_query, query_half) + add_query, query_half)
    out_latent = put_half(out_latent, pick_half(out_latent, query_half) + add_out, query_half)
    start = key_base + key_half * half
    current = lax.dynamic_slice_in_dim(key_terms, start, half, 0)
    key_terms = lax.dynamic_update_slice_in_dim(key_terms, current + term, start, 0)
    return (grad_query, out_latent, key_terms)


def visit_own(carry, visit):
    for query_half, key_half in ((0, 0), (1, 0), (1, 1)):
        carry = visit(carry, query_half, key_half)
    return carry


def visit_block(carry, visit, key_first, own_first):
    carry = visit(carry, 1, 0)
    chosen = jnp.where(key_first < own_first, 0, 1).astype(jnp.int32)
    return visit(carry, chosen, chosen)


def per_device(query_nope, query_rope, latent, grad_out, w_up, block_order):
    tokens = latent.shape[1]
    half = tokens // 2
    blocks = lax.axis_size("blk")
    my_index = lax.axis_index("blk")
    width = LATENT + ROPE_DIM
    weights = lax.all_gather(w_up, "fsdp", axis=0, tiled=True)
    w_key = weights[:, : HEADS * NOPE_DIM].reshape(LATENT, HEADS, NOPE_DIM)
    w_value = weights[:, HEADS * NOPE_DIM :].reshape(LATENT, HEADS, VALUE_DIM)
    nope_rows = query_nope[0].reshape(tokens, HEADS, NOPE_DIM)
    grad_heads = grad_out[0].reshape(tokens, HEADS, VALUE_DIM)
    absorbed = jnp.einsum(
        "thn,jhn->thj", nope_rows, w_key, preferred_element_type=jnp.float32
    ).astype(jnp.bfloat16)
    query_full = jnp.concatenate(
        [absorbed, query_rope[0].reshape(tokens, HEADS, ROPE_DIM)], axis=-1
    )
    grad_absorbed = jnp.einsum(
        "thv,jhv->thj", grad_heads, w_value, preferred_element_type=jnp.float32
    ).astype(jnp.bfloat16)
    own_keys = latent[0]
    offsets = jnp.arange(half, dtype=jnp.int32)
    positions = (block_order[:, :, None] * half + offsets[None, None, :]).reshape(blocks * tokens)
    own_pos = lax.dynamic_slice_in_dim(positions, my_index * tokens, tokens, 0)
    first_blocks = block_order[:, 0]
    own_first = lax.dynamic_index_in_dim(first_blocks, my_index, 0, keepdims=False)
    query_stack = query_full.reshape(2, half, HEADS, width)
    grad_stack = grad_absorbed.reshape(2, half, HEADS, LATENT)
    pos_stack = own_pos.reshape(2, half)
    forward_context = (query_stack, grad_stack, pos_stack)

    def source_of(step):
        source = (my_index - step) % blocks
        held_pos = lax.dynamic_slice_in_dim(positions, source * tokens, tokens, 0)
        key_first = lax.dynamic_index_in_dim(first_blocks, source, 0, keepdims=False)
        return (source, held_pos, key_first)

    stats = (
        jnp.full((2, HEADS, half), NEG_FILL, jnp.float32),
        jnp.zeros((2, HEADS, half), jnp.float32),
        jnp.zeros((2, HEADS, half), jnp.float32),
    )
    stats = visit_own(
        stats,
        lambda carry, query_half, key_half: forward_visit(
            carry, forward_context, own_keys, own_pos, query_half, key_half
        ),
    )

    def forward_turn(step, state):
        held, current = state
        held = circulate(held)
        source, held_pos, key_first = source_of(step)
        current = visit_block(
            current,
            lambda carry, query_half, key_half: forward_visit(
                carry, forward_context, held, held_pos, query_half, key_half
            ),
            key_first,
            own_first,
        )
        return (held, current)

    stats = lax.fori_loop(1, blocks, forward_turn, (own_keys, stats))[1]
    norm_log = stats[0] + jnp.log(stats[1])
    centre = stats[2] / stats[1]
    backward_context = (query_stack, grad_stack, pos_stack, norm_log, centre)
    grad_query = jnp.zeros((2, half, HEADS, width), jnp.float32)
    out_latent = jnp.zeros((2, half, HEADS, LATENT), jnp.float32)
    carry = (grad_query, out_latent, jnp.zeros((tokens, width), jnp.float32))
    carry = visit_own(
        carry,
        lambda inner, query_half, key_half: backward_visit(
            inner, backward_context, own_keys, own_pos, 0, query_half, key_half
        ),
    )

    def backward_turn(step, state):
        held, inner = state
        held = circulate(held)
        inner = (inner[0], inner[1], pass_terms(inner[2]))
        source, held_pos, key_first = source_of(step)
        inner = visit_block(
            inner,
            lambda value, query_half, key_half: backward_visit(
                value, backward_context, held, held_pos, 0, query_half, key_half
            ),
            key_first,
            own_first,
        )
        return (held, inner)

    grad_query, out_latent, key_terms = lax.fori_loop(1, blocks, backward_turn, (own_keys, carry))[
        1
    ]
    latent_grad = pass_terms(key_terms)
    grad_query = grad_query.reshape(tokens, HEADS, width)
    grad_abs_low = grad_query[:, :, :LATENT].astype(jnp.bfloat16)
    grad_rope = grad_query[:, :, LATENT:].astype(jnp.bfloat16).reshape(tokens, HEADS * ROPE_DIM)
    grad_nope = (
        jnp.einsum("thj,jhn->thn", grad_abs_low, w_key, preferred_element_type=jnp.float32)
        .astype(jnp.bfloat16)
        .reshape(tokens, HEADS * NOPE_DIM)
    )
    out_low = out_latent.reshape(tokens, HEADS, LATENT).astype(jnp.bfloat16)
    grad_key_w = jnp.einsum(
        "thj,thn->jhn", grad_abs_low, nope_rows, preferred_element_type=jnp.float32
    ).reshape(LATENT, HEADS * NOPE_DIM)
    grad_value_w = jnp.einsum(
        "thj,thv->jhv", out_low, grad_heads, preferred_element_type=jnp.float32
    ).reshape(LATENT, HEADS * VALUE_DIM)
    weight_terms = jnp.concatenate([grad_key_w, grad_value_w], axis=1)
    grad_up = lax.psum_scatter(weight_terms, ("fsdp", "blk"), scatter_dimension=0, tiled=True)
    return (grad_nope[None], grad_rope[None], latent_grad.astype(jnp.bfloat16)[None], grad_up)


def solution(mesh):
    placed = (
        P("fsdp", "blk", None),
        P("fsdp", "blk", None),
        P("fsdp", "blk", None),
        P("fsdp", "blk", None),
        P("fsdp", None),
        P(),
    )
    return jax.shard_map(
        per_device,
        mesh=mesh,
        in_specs=placed,
        out_specs=(
            P("fsdp", "blk", None),
            P("fsdp", "blk", None),
            P("fsdp", "blk", None),
            P(("fsdp", "blk"), None),
        ),
        check_vma=False,
    )
```

profile of v0, /device:TPU:0, one launch (start us, length us, event | category | flops | bytes accessed | tf_op | source)
XLA Modules:
  0.0 1281.8 jit_solution(14625478793005743799)
XLA Ops:
  14.1 25.2 %all-gather.2.cloned.1.call-done = bf16[512,2048]{0,1:T(8,128)(2,1)} async-done(((bf16[128,2048]{0,1:T(8,128)(2,1)}), bf16[512,2048]{0,1:T(8,128)(2,1)}) %all-gather.2.cloned.1.call-update) | async-done | bytes 2097168 | tf_op jit(solution)/shard_map/all_gather | solution.py:135
  60.4 396.0 %while.42 = (s32[]{:T(128)}, bf16[128,576]{1,0:T(8,128)(2,1)}, f32[2,8,64]{2,1,0:T(8,128)S(1)}, f32[2,8,64]{2,1,0:T(8,128)S(1)}, f32[2,8,64]{2,1,0:T(8,128)S(1)}...) while((s32[]{:T(128)}, bf16[128,576]{1,0:T(8,128)(2,1)}, ...), condition=%wide.region_16.17_spmd, body=%wide.region_9.16_spmd.sunk | while | flops 143274016 | bytes 4751430 | solution.py:192
  64.9 6.5 collective-permute-done
  77.0 7.1 collective-permute-done
  89.7 6.9 collective-permute-done
  102.2 6.9 collective-permute-done
  114.7 6.9 collective-permute-done
  127.1 6.9 collective-permute-done
  139.6 6.9 collective-permute-done
  152.1 6.9 collective-permute-done
  164.6 6.9 collective-permute-done
  177.0 7.8 collective-permute-done
  190.5 8.3 collective-permute-done
  204.4 7.4 collective-permute-done
  217.4 6.9 collective-permute-done
  229.9 6.9 collective-permute-done
  242.3 6.9 collective-permute-done
  254.8 6.9 collective-permute-done
  267.3 6.9 collective-permute-done
  279.8 6.9 collective-permute-done
  292.2 6.9 collective-permute-done
  304.7 7.4 collective-permute-done
  317.7 8.6 collective-permute-done
  331.9 7.8 collective-permute-done
  345.2 7.0 collective-permute-done
  357.8 6.9 collective-permute-done
  370.3 6.9 collective-permute-done
  382.7 6.9 collective-permute-done
  395.2 6.9 collective-permute-done
  407.7 6.9 collective-permute-done
  420.2 6.9 collective-permute-done
  432.6 6.9 collective-permute-done
  445.1 8.5 collective-permute-done
  479.0 626.9 %while.43 = (s32[]{:T(128)}, bf16[128,576]{1,0:T(8,128)(2,1)S(1)}, f32[2,64,8,576]{3,1,2,0:T(8,128)}, f32[2,64,8,512]{3,1,2,0:T(8,128)S(1)}, f32[128,576]{1,0:T(...) while((s32[]{:T(128)}, bf16[128,576]{1,0:T(8,128)(2,1)S(1)}, ...), condition=%wide.region_18.19_spmd, body=%wide.region_17.18_spmd.sunk | while | flops 430342176 | bytes 53637360 | solution.py:221
  484.2 4.3 collective-permute-done.1
  504.6 4.3 collective-permute-done.1
  524.8 4.3 collective-permute-done.1
  545.0 4.3 collective-permute-done.1
  565.2 4.3 collective-permute-done.1
  585.5 4.3 collective-permute-done.1
  605.7 4.3 collective-permute-done.1
  625.9 4.3 collective-permute-done.1
  646.1 4.3 collective-permute-done.1
  666.3 4.3 collective-permute-done.1
  686.5 4.3 collective-permute-done.1
  706.7 4.3 collective-permute-done.1
  726.9 4.3 collective-permute-done.1
  747.1 4.3 collective-permute-done.1
  767.4 4.3 collective-permute-done.1
  787.6 4.3 collective-permute-done.1
  828.0 4.3 collective-permute-done.1
  848.2 4.3 collective-permute-done.1
  888.6 4.3 collective-permute-done.1
  908.8 4.3 collective-permute-done.1
  969.5 4.3 collective-permute-done.1
  989.7 4.3 collective-permute-done.1
  1009.9 4.3 collective-permute-done.1
  1030.1 4.3 collective-permute-done.1
  1050.3 4.3 collective-permute-done.1
  1070.5 4.3 collective-permute-done.1
  1090.7 4.4 collective-permute-done.1
  1117.3 4.7 pad_maximum_fusion
  1125.9 7.1 collective-permute-done.3
  1133.0 139.8 %all-reduce.9.cloned.1.call-done = f32[512,2048]{1,0:T(8,128)} async-done(((f32[512,2048]{1,0:T(8,128)}), f32[512,2048]{1,0:T(8,128)}) %all-reduce.9.cloned.1.call-update) | async-done | bytes 4194320
  (1749 shorter events, 660.2 us)
Async XLA Ops:
  7.2 32.0 %all-gather.2.cloned.1.call-start = ((), (), s32[]{:S(2)}) async-start(), calls=%async_computation | async-start | bytes 2621440 | tf_op jit(solution)/shard_map/all_gather | solution.py:135
  9.4 1263.4 %all-reduce.9.cloned.1.call-start = ((), (), s32[]{:S(2)}) async-start(), calls=%async_computation.1 | async-start | bytes 8388608
  60.6 10.9 collective-permute-start
  74.1 10.0 collective-permute-start
  86.8 9.7 collective-permute-start
  99.3 9.7 collective-permute-start
  111.8 9.7 collective-permute-start
  124.3 9.7 collective-permute-start
  136.8 9.7 collective-permute-start
  149.2 9.7 collective-permute-start
  161.7 9.7 collective-permute-start
  174.2 10.7 collective-permute-start
  187.6 11.2 collective-permute-start
  201.5 10.3 collective-permute-start
  214.5 9.7 collective-permute-start
  227.0 9.7 collective-permute-start
  239.5 9.7 collective-permute-start
  252.0 9.7 collective-permute-start
  264.4 9.7 collective-permute-start
  276.9 9.7 collective-permute-start
  289.4 9.7 collective-permute-start
  301.9 10.3 collective-permute-start
  314.9 11.4 collective-permute-start
  329.0 10.7 collective-permute-start
  342.4 9.8 collective-permute-start
  354.9 9.7 collective-permute-start
  367.4 9.7 collective-permute-start
  379.9 9.7 collective-permute-start
  392.4 9.7 collective-permute-start
  404.8 9.7 collective-permute-start
  417.3 9.7 collective-permute-start
  429.8 9.7 collective-permute-start
  442.3 11.4 collective-permute-start
  479.0 14.8 %collective-permute-start.2 = (f32[128,576]{1,0:T(8,128)}, f32[128,576]{1,0:T(8,128)}, u32[]{:S(2)}, u32[]{:S(2)}) collective-permute-start(f32[128,576]{1,0:T(8,128)} %get-tuple-element.1207), channel_id=1, source_target_pairs={{31,0},{0,1},{1,2},{2,3},{3,4},{4,5},{5,6},{6,7},{7,8},{8,9},{9,10... | collective-permute-start | bytes 884744 | tf_op jit(solution)/shard_map/while/body/eval_jaxpr/ppermute | solution.py:21
  499.4 14.5 %collective-permute-start.2 = (f32[128,576]{1,0:T(8,128)}, f32[128,576]{1,0:T(8,128)}, u32[]{:S(2)}, u32[]{:S(2)}) collective-permute-start(f32[128,576]{1,0:T(8,128)} %get-tuple-element.1207), channel_id=1, source_target_pairs={{31,0},{0,1},{1,2},{2,3},{3,4},{4,5},{5,6},{6,7},{7,8},{8,9},{9,10... | collective-permute-start | bytes 884744 | tf_op jit(solution)/shard_map/while/body/eval_jaxpr/ppermute | solution.py:21
  519.6 14.5 %collective-permute-start.2 = (f32[128,576]{1,0:T(8,128)}, f32[128,576]{1,0:T(8,128)}, u32[]{:S(2)}, u32[]{:S(2)}) collective-permute-start(f32[128,576]{1,0:T(8,128)} %get-tuple-element.1207), channel_id=1, source_target_pairs={{31,0},{0,1},{1,2},{2,3},{3,4},{4,5},{5,6},{6,7},{7,8},{8,9},{9,10... | collective-permute-start | bytes 884744 | tf_op jit(solution)/shard_map/while/body/eval_jaxpr/ppermute | solution.py:21
  539.8 14.5 %collective-permute-start.2 = (f32[128,576]{1,0:T(8,128)}, f32[128,576]{1,0:T(8,128)}, u32[]{:S(2)}, u32[]{:S(2)}) collective-permute-start(f32[128,576]{1,0:T(8,128)} %get-tuple-element.1207), channel_id=1, source_target_pairs={{31,0},{0,1},{1,2},{2,3},{3,4},{4,5},{5,6},{6,7},{7,8},{8,9},{9,10... | collective-permute-start | bytes 884744 | tf_op jit(solution)/shard_map/while/body/eval_jaxpr/ppermute | solution.py:21
  560.0 14.5 %collective-permute-start.2 = (f32[128,576]{1,0:T(8,128)}, f32[128,576]{1,0:T(8,128)}, u32[]{:S(2)}, u32[]{:S(2)}) collective-permute-start(f32[128,576]{1,0:T(8,128)} %get-tuple-element.1207), channel_id=1, source_target_pairs={{31,0},{0,1},{1,2},{2,3},{3,4},{4,5},{5,6},{6,7},{7,8},{8,9},{9,10... | collective-permute-start | bytes 884744 | tf_op jit(solution)/shard_map/while/body/eval_jaxpr/ppermute | solution.py:21
  580.2 14.5 %collective-permute-start.2 = (f32[128,576]{1,0:T(8,128)}, f32[128,576]{1,0:T(8,128)}, u32[]{:S(2)}, u32[]{:S(2)}) collective-permute-start(f32[128,576]{1,0:T(8,128)} %get-tuple-element.1207), channel_id=1, source_target_pairs={{31,0},{0,1},{1,2},{2,3},{3,4},{4,5},{5,6},{6,7},{7,8},{8,9},{9,10... | collective-permute-start | bytes 884744 | tf_op jit(solution)/shard_map/while/body/eval_jaxpr/ppermute | solution.py:21
  600.5 14.5 %collective-permute-start.2 = (f32[128,576]{1,0:T(8,128)}, f32[128,576]{1,0:T(8,128)}, u32[]{:S(2)}, u32[]{:S(2)}) collective-permute-start(f32[128,576]{1,0:T(8,128)} %get-tuple-element.1207), channel_id=1, source_target_pairs={{31,0},{0,1},{1,2},{2,3},{3,4},{4,5},{5,6},{6,7},{7,8},{8,9},{9,10... | collective-permute-start | bytes 884744 | tf_op jit(solution)/shard_map/while/body/eval_jaxpr/ppermute | solution.py:21
  620.7 14.5 %collective-permute-start.2 = (f32[128,576]{1,0:T(8,128)}, f32[128,576]{1,0:T(8,128)}, u32[]{:S(2)}, u32[]{:S(2)}) collective-permute-start(f32[128,576]{1,0:T(8,128)} %get-tuple-element.1207), channel_id=1, source_target_pairs={{31,0},{0,1},{1,2},{2,3},{3,4},{4,5},{5,6},{6,7},{7,8},{8,9},{9,10... | collective-permute-start | bytes 884744 | tf_op jit(solution)/shard_map/while/body/eval_jaxpr/ppermute | solution.py:21
  640.9 14.5 %collective-permute-start.2 = (f32[128,576]{1,0:T(8,128)}, f32[128,576]{1,0:T(8,128)}, u32[]{:S(2)}, u32[]{:S(2)}) collective-permute-start(f32[128,576]{1,0:T(8,128)} %get-tuple-element.1207), channel_id=1, source_target_pairs={{31,0},{0,1},{1,2},{2,3},{3,4},{4,5},{5,6},{6,7},{7,8},{8,9},{9,10... | collective-permute-start | bytes 884744 | tf_op jit(solution)/shard_map/while/body/eval_jaxpr/ppermute | solution.py:21
  661.1 14.5 %collective-permute-start.2 = (f32[128,576]{1,0:T(8,128)}, f32[128,576]{1,0:T(8,128)}, u32[]{:S(2)}, u32[]{:S(2)}) collective-permute-start(f32[128,576]{1,0:T(8,128)} %get-tuple-element.1207), channel_id=1, source_target_pairs={{31,0},{0,1},{1,2},{2,3},{3,4},{4,5},{5,6},{6,7},{7,8},{8,9},{9,10... | collective-permute-start | bytes 884744 | tf_op jit(solution)/shard_map/while/body/eval_jaxpr/ppermute | solution.py:21
  681.3 14.5 %collective-permute-start.2 = (f32[128,576]{1,0:T(8,128)}, f32[128,576]{1,0:T(8,128)}, u32[]{:S(2)}, u32[]{:S(2)}) collective-permute-start(f32[128,576]{1,0:T(8,128)} %get-tuple-element.1207), channel_id=1, source_target_pairs={{31,0},{0,1},{1,2},{2,3},{3,4},{4,5},{5,6},{6,7},{7,8},{8,9},{9,10... | collective-permute-start | bytes 884744 | tf_op jit(solution)/shard_map/while/body/eval_jaxpr/ppermute | solution.py:21
  701.5 14.5 %collective-permute-start.2 = (f32[128,576]{1,0:T(8,128)}, f32[128,576]{1,0:T(8,128)}, u32[]{:S(2)}, u32[]{:S(2)}) collective-permute-start(f32[128,576]{1,0:T(8,128)} %get-tuple-element.1207), channel_id=1, source_target_pairs={{31,0},{0,1},{1,2},{2,3},{3,4},{4,5},{5,6},{6,7},{7,8},{8,9},{9,10... | collective-permute-start | bytes 884744 | tf_op jit(solution)/shard_map/while/body/eval_jaxpr/ppermute | solution.py:21
  721.7 14.5 %collective-permute-start.2 = (f32[128,576]{1,0:T(8,128)}, f32[128,576]{1,0:T(8,128)}, u32[]{:S(2)}, u32[]{:S(2)}) collective-permute-start(f32[128,576]{1,0:T(8,128)} %get-tuple-element.1207), channel_id=1, source_target_pairs={{31,0},{0,1},{1,2},{2,3},{3,4},{4,5},{5,6},{6,7},{7,8},{8,9},{9,10... | collective-permute-start | bytes 884744 | tf_op jit(solution)/shard_map/while/body/eval_jaxpr/ppermute | solution.py:21
  741.9 14.5 %collective-permute-start.2 = (f32[128,576]{1,0:T(8,128)}, f32[128,576]{1,0:T(8,128)}, u32[]{:S(2)}, u32[]{:S(2)}) collective-permute-start(f32[128,576]{1,0:T(8,128)} %get-tuple-element.1207), channel_id=1, source_target_pairs={{31,0},{0,1},{1,2},{2,3},{3,4},{4,5},{5,6},{6,7},{7,8},{8,9},{9,10... | collective-permute-start | bytes 884744 | tf_op jit(solution)/shard_map/while/body/eval_jaxpr/ppermute | solution.py:21
  762.1 14.5 %collective-permute-start.2 = (f32[128,576]{1,0:T(8,128)}, f32[128,576]{1,0:T(8,128)}, u32[]{:S(2)}, u32[]{:S(2)}) collective-permute-start(f32[128,576]{1,0:T(8,128)} %get-tuple-element.1207), channel_id=1, source_target_pairs={{31,0},{0,1},{1,2},{2,3},{3,4},{4,5},{5,6},{6,7},{7,8},{8,9},{9,10... | collective-permute-start | bytes 884744 | tf_op jit(solution)/shard_map/while/body/eval_jaxpr/ppermute | solution.py:21
  782.3 14.5 %collective-permute-start.2 = (f32[128,576]{1,0:T(8,128)}, f32[128,576]{1,0:T(8,128)}, u32[]{:S(2)}, u32[]{:S(2)}) collective-permute-start(f32[128,576]{1,0:T(8,128)} %get-tuple-element.1207), channel_id=1, source_target_pairs={{31,0},{0,1},{1,2},{2,3},{3,4},{4,5},{5,6},{6,7},{7,8},{8,9},{9,10... | collective-permute-start | bytes 884744 | tf_op jit(solution)/shard_map/while/body/eval_jaxpr/ppermute | solution.py:21
  802.6 14.5 %collective-permute-start.2 = (f32[128,576]{1,0:T(8,128)}, f32[128,576]{1,0:T(8,128)}, u32[]{:S(2)}, u32[]{:S(2)}) collective-permute-start(f32[128,576]{1,0:T(8,128)} %get-tuple-element.1207), channel_id=1, source_target_pairs={{31,0},{0,1},{1,2},{2,3},{3,4},{4,5},{5,6},{6,7},{7,8},{8,9},{9,10... | collective-permute-start | bytes 884744 | tf_op jit(solution)/shard_map/while/body/eval_jaxpr/ppermute | solution.py:21
  822.8 14.5 %collective-permute-start.2 = (f32[128,576]{1,0:T(8,128)}, f32[128,576]{1,0:T(8,128)}, u32[]{:S(2)}, u32[]{:S(2)}) collective-permute-start(f32[128,576]{1,0:T(8,128)} %get-tuple-element.1207), channel_id=1, source_target_pairs={{31,0},{0,1},{1,2},{2,3},{3,4},{4,5},{5,6},{6,7},{7,8},{8,9},{9,10... | collective-permute-start | bytes 884744 | tf_op jit(solution)/shard_map/while/body/eval_jaxpr/ppermute | solution.py:21
  843.0 14.5 %collective-permute-start.2 = (f32[128,576]{1,0:T(8,128)}, f32[128,576]{1,0:T(8,128)}, u32[]{:S(2)}, u32[]{:S(2)}) collective-permute-start(f32[128,576]{1,0:T(8,128)} %get-tuple-element.1207), channel_id=1, source_target_pairs={{31,0},{0,1},{1,2},{2,3},{3,4},{4,5},{5,6},{6,7},{7,8},{8,9},{9,10... | collective-permute-start | bytes 884744 | tf_op jit(solution)/shard_map/while/body/eval_jaxpr/ppermute | solution.py:21
  863.2 14.5 %collective-permute-start.2 = (f32[128,576]{1,0:T(8,128)}, f32[128,576]{1,0:T(8,128)}, u32[]{:S(2)}, u32[]{:S(2)}) collective-permute-start(f32[128,576]{1,0:T(8,128)} %get-tuple-element.1207), channel_id=1, source_target_pairs={{31,0},{0,1},{1,2},{2,3},{3,4},{4,5},{5,6},{6,7},{7,8},{8,9},{9,10... | collective-permute-start | bytes 884744 | tf_op jit(solution)/shard_map/while/body/eval_jaxpr/ppermute | solution.py:21
  883.4 14.5 %collective-permute-start.2 = (f32[128,576]{1,0:T(8,128)}, f32[128,576]{1,0:T(8,128)}, u32[]{:S(2)}, u32[]{:S(2)}) collective-permute-start(f32[128,576]{1,0:T(8,128)} %get-tuple-element.1207), channel_id=1, source_target_pairs={{31,0},{0,1},{1,2},{2,3},{3,4},{4,5},{5,6},{6,7},{7,8},{8,9},{9,10... | collective-permute-start | bytes 884744 | tf_op jit(solution)/shard_map/while/body/eval_jaxpr/ppermute | solution.py:21
  903.6 14.5 %collective-permute-start.2 = (f32[128,576]{1,0:T(8,128)}, f32[128,576]{1,0:T(8,128)}, u32[]{:S(2)}, u32[]{:S(2)}) collective-permute-start(f32[128,576]{1,0:T(8,128)} %get-tuple-element.1207), channel_id=1, source_target_pairs={{31,0},{0,1},{1,2},{2,3},{3,4},{4,5},{5,6},{6,7},{7,8},{8,9},{9,10... | collective-permute-start | bytes 884744 | tf_op jit(solution)/shard_map/while/body/eval_jaxpr/ppermute | solution.py:21
  923.8 14.5 %collective-permute-start.2 = (f32[128,576]{1,0:T(8,128)}, f32[128,576]{1,0:T(8,128)}, u32[]{:S(2)}, u32[]{:S(2)}) collective-permute-start(f32[128,576]{1,0:T(8,128)} %get-tuple-element.1207), channel_id=1, source_target_pairs={{31,0},{0,1},{1,2},{2,3},{3,4},{4,5},{5,6},{6,7},{7,8},{8,9},{9,10... | collective-permute-start | bytes 884744 | tf_op jit(solution)/shard_map/while/body/eval_jaxpr/ppermute | solution.py:21
  944.0 14.5 %collective-permute-start.2 = (f32[128,576]{1,0:T(8,128)}, f32[128,576]{1,0:T(8,128)}, u32[]{:S(2)}, u32[]{:S(2)}) collective-permute-start(f32[128,576]{1,0:T(8,128)} %get-tuple-element.1207), channel_id=1, source_target_pairs={{31,0},{0,1},{1,2},{2,3},{3,4},{4,5},{5,6},{6,7},{7,8},{8,9},{9,10... | collective-permute-start | bytes 884744 | tf_op jit(solution)/shard_map/while/body/eval_jaxpr/ppermute | solution.py:21
  964.2 14.5 %collective-permute-start.2 = (f32[128,576]{1,0:T(8,128)}, f32[128,576]{1,0:T(8,128)}, u32[]{:S(2)}, u32[]{:S(2)}) collective-permute-start(f32[128,576]{1,0:T(8,128)} %get-tuple-element.1207), channel_id=1, source_target_pairs={{31,0},{0,1},{1,2},{2,3},{3,4},{4,5},{5,6},{6,7},{7,8},{8,9},{9,10... | collective-permute-start | bytes 884744 | tf_op jit(solution)/shard_map/while/body/eval_jaxpr/ppermute | solution.py:21
  984.5 14.5 %collective-permute-start.2 = (f32[128,576]{1,0:T(8,128)}, f32[128,576]{1,0:T(8,128)}, u32[]{:S(2)}, u32[]{:S(2)}) collective-permute-start(f32[128,576]{1,0:T(8,128)} %get-tuple-element.1207), channel_id=1, source_target_pairs={{31,0},{0,1},{1,2},{2,3},{3,4},{4,5},{5,6},{6,7},{7,8},{8,9},{9,10... | collective-permute-start | bytes 884744 | tf_op jit(solution)/shard_map/while/body/eval_jaxpr/ppermute | solution.py:21
  1004.7 14.5 %collective-permute-start.2 = (f32[128,576]{1,0:T(8,128)}, f32[128,576]{1,0:T(8,128)}, u32[]{:S(2)}, u32[]{:S(2)}) collective-permute-start(f32[128,576]{1,0:T(8,128)} %get-tuple-element.1207), channel_id=1, source_target_pairs={{31,0},{0,1},{1,2},{2,3},{3,4},{4,5},{5,6},{6,7},{7,8},{8,9},{9,10... | collective-permute-start | bytes 884744 | tf_op jit(solution)/shard_map/while/body/eval_jaxpr/ppermute | solution.py:21
  1024.9 14.5 %collective-permute-start.2 = (f32[128,576]{1,0:T(8,128)}, f32[128,576]{1,0:T(8,128)}, u32[]{:S(2)}, u32[]{:S(2)}) collective-permute-start(f32[128,576]{1,0:T(8,128)} %get-tuple-element.1207), channel_id=1, source_target_pairs={{31,0},{0,1},{1,2},{2,3},{3,4},{4,5},{5,6},{6,7},{7,8},{8,9},{9,10... | collective-permute-start | bytes 884744 | tf_op jit(solution)/shard_map/while/body/eval_jaxpr/ppermute | solution.py:21
  1045.1 14.5 %collective-permute-start.2 = (f32[128,576]{1,0:T(8,128)}, f32[128,576]{1,0:T(8,128)}, u32[]{:S(2)}, u32[]{:S(2)}) collective-permute-start(f32[128,576]{1,0:T(8,128)} %get-tuple-element.1207), channel_id=1, source_target_pairs={{31,0},{0,1},{1,2},{2,3},{3,4},{4,5},{5,6},{6,7},{7,8},{8,9},{9,10... | collective-permute-start | bytes 884744 | tf_op jit(solution)/shard_map/while/body/eval_jaxpr/ppermute | solution.py:21
  1065.3 14.5 %collective-permute-start.2 = (f32[128,576]{1,0:T(8,128)}, f32[128,576]{1,0:T(8,128)}, u32[]{:S(2)}, u32[]{:S(2)}) collective-permute-start(f32[128,576]{1,0:T(8,128)} %get-tuple-element.1207), channel_id=1, source_target_pairs={{31,0},{0,1},{1,2},{2,3},{3,4},{4,5},{5,6},{6,7},{7,8},{8,9},{9,10... | collective-permute-start | bytes 884744 | tf_op jit(solution)/shard_map/while/body/eval_jaxpr/ppermute | solution.py:21
  1085.5 14.7 %collective-permute-start.2 = (f32[128,576]{1,0:T(8,128)}, f32[128,576]{1,0:T(8,128)}, u32[]{:S(2)}, u32[]{:S(2)}) collective-permute-start(f32[128,576]{1,0:T(8,128)} %get-tuple-element.1207), channel_id=1, source_target_pairs={{31,0},{0,1},{1,2},{2,3},{3,4},{4,5},{5,6},{6,7},{7,8},{8,9},{9,10... | collective-permute-start | bytes 884744 | tf_op jit(solution)/shard_map/while/body/eval_jaxpr/ppermute | solution.py:21
  (172 other events, 962.7 us)
Sparse Core Ops, SparseCore 0:
  9.7 29.4 all-gather.1
  1122.1 150.6 all-reduce.8
where the time goes:
time: 1290 us; the launch traced here: 1280 us
  waiting for transfers between devices  527 us (41%)
  matrix products  314 us (24%)
  local copies, waits for them, and re-layouts  306 us (24%)
  loops' own time  92.5 us (7%)
  other arithmetic  24.5 us (2%)
  between operations  14.7 us (1%)
    ppermute x94, waiting for transfers between devices, from_behind(): return lax.ppermute(block, axis, route)  363 us
    unnamed x3, waiting for transfers between devices  140 us
    dot_general x65, matrix products, backward_visit(): jnp.einsum('htu,thk->uk', grad_low, query_rows, preferred_element_type=jn...  123 us
    while x279, local copies, waits for them, and re-layouts  106 us
    dot_general x127, matrix products, masked_scores(): jnp.einsum('thk,uk->htu', query_rows, key_rows, preferred_element_type=jn...  69.4 us
    dynamic_slice x62, local copies, waits for them, and re-layouts, source_of(): lax.dynamic_index_in_dim(first_blocks, source, 0, keepdims=False)  56.9 us
    dynamic_slice x126, local copies, waits for them, and re-layouts, pick_half(): return lax.dynamic_index_in_dim(stacked, which, 0, keepdims=False)  54.6 us
    another operation x1, loops' own time, per_device(): lax.fori_loop(1, blocks, backward_turn, (own_keys, carry))[1]  47.7 us
  transfers between devices with their start and end apart: 96, of which 67 were waited for; matrix products, arithmetic and copies ran while one was open for 23% of the time, Pallas kernels for 0%

commit v1 on v0

v1 whole, which is shorter than its diff:
```python
import functools
import math

import jax
import jax.numpy as jnp
from jax import lax
from jax.experimental import pallas as pl
from jax.experimental.pallas import tpu as pltpu
from jax.sharding import PartitionSpec as P

HEADS = 8
LATENT = 512
SCALE = 1.0 / math.sqrt(192.0)
NEG_FILL = -1e30
F32 = jnp.float32
BF16 = jnp.bfloat16
MESH = pl.DeviceIdType.MESH
COPIES = 112


def mm(a, b):
    return lax.dot_general(a, b, (((1,), (0,)), ((), ())), preferred_element_type=F32)


def mm_nt(a, b):
    return lax.dot_general(a, b, (((1,), (1,)), ((), ())), preferred_element_type=F32)


def add_into(ref, *others):
    total = ref[...].astype(F32)
    for other in others:
        total = total + other[...].astype(F32)
    ref[...] = total.astype(BF16)


def kernel(
    order, lat, nope_o, rope_o, gout_o, w_own,
    gn_out, gr_out, gl_out, gu_out,
    kbuf, keys, keys_t, nope_p, rope_p, gout_p, w_all, wk_t,
    query, grad, probs, gprob, gscore, peaks, peak, total, centre, stat_s, stat_r,
    dq_t, out_t, gn_own, gn_send, gn_recv, ro_recv,
    dkb, ra1, ra2, ra3, ra4, rb1, rb2, rb3, rb4,
    up, uc, uzs, uz, us1, upr, us2, uyr, us3, uxr,
    send, recv,
):
    f = lax.axis_index("fsdp")
    blk = lax.axis_index("blk")
    x, zl, y = blk % 4, (blk // 4) % 2, blk // 8
    xp, xm, x2 = (x + 1) % 4, (x + 3) % 4, (x + 2) % 4
    yp, ym, y2 = (y + 1) % 4, (y + 3) % 4, (y + 2) % 4
    f1 = f + 1 - 2 * (f % 2)
    f2 = (f + 2) % 4
    f3 = (f1 + 2) % 4

    def at(yy, xx):
        return {"blk": (yy * 2 + zl) * 4 + xx}

    to_xp, to_xm, to_x2 = at(y, xp), at(y, xm), at(y, x2)
    to_yp, to_ym, to_y2 = at(yp, x), at(ym, x), at(y2, x)
    to_pair = {"blk": blk + 4 - 8 * zl}
    to_core = {"fsdp": f1}
    to_far = {"fsdp": f2, "blk": blk + 4 - 8 * zl}

    made = {}

    def define(name, src, dst, device):
        number = len(made)
        made[name] = lambda: pltpu.make_async_remote_copy(
            src_ref=src(), dst_ref=dst(), send_sem=send.at[number], recv_sem=recv.at[number],
            device_id=device, device_id_type=MESH,
        )

    def start(*names):
        for name in names:
            made[name]().start()

    def wait(*names):
        for name in names:
            made[name]().wait_recv()

    def key_part(yy, xx, first, count):
        return lambda: kbuf.at[yy * 4 + xx, pl.ds(first, count)]

    def same(name, part, device):
        define(name, part, part, device)

    for name, first, count, cut, swap in (("a", 0, 80, 48, False), ("b", 80, 64, 32, True)):
        def part(dy, dx, first=first, count=count, swap=swap):
            if swap:
                dy, dx = dx, dy
            return key_part((y + dy) % 4, (x + dx) % 4, first, count)

        ip, im, jp, jm = (to_yp, to_ym, to_xp, to_xm) if swap else (to_xp, to_xm, to_yp, to_ym)
        same(name + "1", part(0, 0), ip)
        same(name + "2", part(0, 0), im)
        same(name + "3", part(0, 0), jp)
        same(name + "4", part(0, 0), jm)
        same(name + "5", part(0, 3, first, cut), ip)
        same(name + "6", part(0, 1, first + cut, count - cut), im)
        same(name + "7", part(0, 3), jp)
        same(name + "8", part(0, 3), jm)
        same(name + "9", part(0, 1), jp)
        same(name + "10", part(0, 1), jm)
        same(name + "11", part(0, 2), jp)
        same(name + "12", part(0, 2), jm)
        same(name + "13", part(3, 0), jp)
        same(name + "14", part(3, 3), jp)
        same(name + "15", part(1, 1), jm)
        same(name + "16", part(1, 2), jm)

    define("qn", lambda: nope_o, lambda: nope_p, to_pair)
    define("qr", lambda: rope_o, lambda: rope_p, to_pair)
    define("qg", lambda: gout_o, lambda: gout_p, to_pair)
    define("w1", lambda: w_own, lambda: w_all.at[f], to_core)
    define("w2", lambda: w_own, lambda: w_all.at[f], to_far)
    define("w3", lambda: w_all.at[f2], lambda: w_all.at[f2], to_core)
    define("st", lambda: stat_s, lambda: stat_r, to_pair)
    define("gn", lambda: gn_send, lambda: gn_recv, to_pair)
    define("ro1", lambda: dq_t.at[1, pl.ds(512, 64)], lambda: ro_recv.at[0], to_pair)
    define("ro3", lambda: dq_t.at[3, pl.ds(512, 64)], lambda: ro_recv.at[1], to_pair)

    def terms(yy, xx, first, count):
        return lambda: dkb.at[yy, xx, pl.ds(first, count)]

    def term_rows(yy, x_first, x_count):
        return lambda: dkb.at[yy, pl.ds(x_first, x_count), pl.ds(0, 80)]

    define("A1p", term_rows(y2, 0, 2), lambda: ra1.at[0], to_yp)
    define("A1m", term_rows(y2, 2, 2), lambda: ra1.at[1], to_ym)
    define("A2p", term_rows(yp, 0, 4), lambda: ra2.at[0], to_yp)
    define("A2m", term_rows(ym, 0, 4), lambda: ra2.at[1], to_ym)
    define("A3p", terms(y, x2, 0, 48), lambda: ra3.at[pl.ds(0, 48)], to_xp)
    define("A3m", terms(y, x2, 48, 32), lambda: ra3.at[pl.ds(48, 32)], to_xm)
    define("A4p", terms(y, xp, 0, 80), lambda: ra4.at[0], to_xp)
    define("A4m", terms(y, xm, 0, 80), lambda: ra4.at[1], to_xm)
    turns = (y2, yp, ym, y)
    for i in range(4):
        define(f"B1{i}", terms(turns[i], x2, 80, 64), lambda i=i: rb1.at[i], to_xp if i % 2 == 0 else to_xm)
        define(f"B2p{i}", terms(turns[i], xp, 80, 64), lambda i=i: rb2.at[i, 0], to_xp)
        define(f"B2m{i}", terms(turns[i], xm, 80, 64), lambda i=i: rb2.at[i, 1], to_xm)
    define("B3p", terms(y2, x, 80, 32), lambda: rb3.at[0], to_yp)
    define("B3m", terms(y2, x, 112, 32), lambda: rb3.at[1], to_ym)
    define("B4p", terms(yp, x, 80, 64), lambda: rb4.at[0], to_yp)
    define("B4m", terms(ym, x, 80, 64), lambda: rb4.at[1], to_ym)

    for i in range(2):
        define(f"C0{i}", lambda i=i: up.at[i, f1], lambda i=i: uc.at[i, 0], to_core)
        define(f"C1{i}", lambda i=i: up.at[i, f3], lambda i=i: uc.at[i, 1], to_core)
        define(f"Z{i}", lambda i=i: uzs.at[i], lambda i=i: uz.at[i], to_far)
        define(f"P{i}", lambda i=i: us1.at[i, :, 1 - zl], lambda i=i: upr.at[i], to_pair)
        define(f"Yp{i}", lambda i=i: us2.at[i, yp], lambda i=i: uyr.at[i, 0], to_yp)
        define(f"Ym{i}", lambda i=i: us2.at[i, ym], lambda i=i: uyr.at[i, 1], to_ym)
        define(f"Y2{i}", lambda i=i: us2.at[i, y2], lambda i=i: uyr.at[i, 2], to_y2)
        define(f"Xp{i}", lambda i=i: us3.at[i], lambda i=i: uxr.at[i, 0], to_xp)
        define(f"Xm{i}", lambda i=i: us3.at[i], lambda i=i: uxr.at[i, 1], to_xm)
        define(f"X2{i}", lambda i=i: us3.at[i], lambda i=i: uxr.at[i, 2], to_x2)

    mine = y * 4 + x
    kbuf[mine, 0:64] = lat[0:64, 0:512]
    kbuf[mine, 80:144] = lat[64:128, 0:512]
    kbuf[mine, 64:80] = jnp.concatenate([lat[s * 16 : s * 16 + 16, 512:576] for s in range(8)], axis=1)
    barrier = pltpu.get_barrier_semaphore()
    partners = (to_xp, to_xm, to_x2, to_yp, to_ym, to_y2, to_pair, to_core, to_far)
    for partner in partners:
        pl.semaphore_signal(barrier, inc=1, device_id=partner, device_id_type=MESH)
    pl.semaphore_wait(barrier, len(partners))

    start("w2", "qn", "a1", "a2", "b1", "b2", "a3", "a4", "b3", "b4", "w1", "qg", "qr")
    w_all[f] = w_own[...]
    for g in range(4):
        query[g, :, 512:640] = jnp.zeros((512, 128), BF16)
    for t in range(8):
        keys[t, :, 512:640] = jnp.zeros((256, 128), BF16)
    for name in ("a", "b"):
        wait(name + "1")
        start(name + "5", name + "7", name + "8")
    for name in ("a", "b"):
        wait(name + "2")
        start(name + "6", name + "9", name + "10")
    for name in ("a", "b"):
        wait(name + "5", name + "6")
        start(name + "11", name + "12")
    for name in ("a", "b"):
        wait(name + "3")
        start(name + "13")
    for name in ("a", "b"):
        wait(name + "7")
        start(name + "14")
    for name in ("a", "b"):
        wait(name + "10")
        start(name + "15")
    for name in ("a", "b"):
        wait(name + "12")
        start(name + "16")

    def project(shard, nope, gout, low, high):
        columns = pl.ds(pl.multiple_of(shard * 128, 128), 128)

        def head(h, _):
            lanes = pl.ds(pl.multiple_of(h * 128, 128), 128)
            value_lanes = pl.ds(pl.multiple_of(1024 + h * 128, 128), 128)
            rows = pl.ds(pl.multiple_of(h * 64, 64), 64)
            a = mm_nt(nope[:, lanes], w_all[shard, :, lanes]).astype(BF16)
            query[low, rows, columns] = a[:64]
            query[high, rows, columns] = a[64:]
            b = mm_nt(gout[:, lanes], w_all[shard, :, value_lanes]).astype(BF16)
            grad[low, rows, columns] = b[:64]
            grad[high, rows, columns] = b[64:]
            return 0

        lax.fori_loop(0, HEADS, head, 0)

    def place_rope(rope, low, high):
        for h in range(HEADS):
            part = rope[:, h * 64 : h * 64 + 64]
            query[low, h * 64 : h * 64 + 64, 512:576] = part[:64]
            query[high, h * 64 : h * 64 + 64, 512:576] = part[64:]

    project(f, nope_o, gout_o, 2, 0)
    place_rope(rope_o, 2, 0)
    wait("w1")
    project(f1, nope_o, gout_o, 2, 0)
    wait("w2")
    start("w3")
    project(f2, nope_o, gout_o, 2, 0)
    wait("qn", "qg", "qr")
    place_rope(rope_p, 3, 1)
    project(f, nope_p, gout_p, 3, 1)
    project(f1, nope_p, gout_p, 3, 1)
    project(f2, nope_p, gout_p, 3, 1)
    wait("w3")
    project(f3, nope_o, gout_o, 2, 0)
    project(f3, nope_p, gout_p, 3, 1)

    for name in ("a", "b"):
        wait(*(name + n for n in ("4", "8", "9", "11", "13", "14", "15", "16")))

    def assemble(p, _):
        yy, xx = p // 4, p % 4
        rows = pl.ds(pl.multiple_of(xx * 64, 64), 64)
        keys[yy, rows, 0:512] = kbuf[p, 0:64]
        keys[4 + yy, rows, 0:512] = kbuf[p, 80:144]
        packed = kbuf[p, 64:80]
        low = jnp.concatenate([packed[:, s * 64 : s * 64 + 64] for s in range(4)], axis=0)
        high = jnp.concatenate([packed[:, s * 64 : s * 64 + 64] for s in range(4, 8)], axis=0)
        keys[yy, rows, 512:576] = low
        keys[4 + yy, rows, 512:576] = high
        return 0

    lax.fori_loop(0, 16, assemble, 0)

    peak[...] = jnp.full((4, 1, 512), NEG_FILL, F32)
    total[...] = jnp.zeros((4, 1, 512), F32)
    centre[...] = jnp.zeros((4, 1, 512), F32)
    own_first = order[blk, 0]
    pair_first = order[blk + 4 - 8 * zl, 0]
    relative = lax.broadcasted_iota(jnp.int32, (64, 512), 0) - lax.broadcasted_iota(jnp.int32, (64, 512), 1) % 64

    def visit(t, g, high, masked):
        tile = 4 + t if high else t
        slot = 16 + g * 4 + t if high else g * 4 + t
        scores = mm_nt(keys[tile], query[g])
        grad_probs = mm_nt(keys[tile, :, 0:512], grad[g])
        if masked:
            first = jnp.where(g % 2 == 0, own_first, pair_first)
            block = 63 - first if high else first
            parts = []
            for xx in range(4):
                key_first = order[(t * 2 + zl) * 4 + xx, 0]
                key_block = 63 - key_first if high else key_first
                parts.append(relative <= (block - key_block) * 64)
            allowed = jnp.concatenate(parts, axis=0)
            scores = jnp.where(allowed, scores, NEG_FILL)
        old = peak[g]
        new = jnp.maximum(old, jnp.max(scores, axis=0, keepdims=True))
        weights = jnp.exp((scores - new) * SCALE)
        if masked:
            weights = jnp.where(allowed, weights, 0.0)
        factor = jnp.exp((old - new) * SCALE)
        total[g] = total[g] * factor + jnp.sum(weights, axis=0, keepdims=True)
        centre[g] = centre[g] * factor + jnp.sum(weights * grad_probs, axis=0, keepdims=True)
        peak[g] = new
        probs[slot] = weights.astype(BF16)
        gprob[slot] = grad_probs
        peaks[slot] = new

    def open_low(i, _):
        visit(i // 2, i % 2, False, False)
        return 0

    def masked_low(i, _):
        visit(i // 2, 2 + i % 2, False, True)
        return 0

    def masked_high(i, _):
        visit(i // 2, i % 2, True, True)
        return 0

    lax.fori_loop(0, 8, open_low, 0)
    lax.fori_loop(0, 8, masked_low, 0)
    lax.fori_loop(0, 8, masked_high, 0)

    for g in range(4):
        stat_s[g, 0:1] = peak[g]
        stat_s[g, 1:2] = total[g]
        stat_s[g, 2:3] = centre[g]
    start("st")
    for t in range(8):
        keys_t[:, t * 256 : t * 256 + 256] = jnp.transpose(keys[t])
    for s in range(4):
        wk_t[:, s * 128 : s * 128 + 128] = jnp.transpose(w_all[s, :, 0:1024])
    wait("st")
    for g in range(4):
        other = g + 1 - 2 * (g % 2)
        here, there = stat_s[g], stat_r[other]
        new = jnp.maximum(here[0:1], there[0:1])
        f_here = jnp.exp((here[0:1] - new) * SCALE)
        f_there = jnp.exp((there[0:1] - new) * SCALE)
        norm = here[1:2] * f_here + there[1:2] * f_there
        peak[g] = new
        total[g] = norm
        centre[g] = (here[2:3] * f_here + there[2:3] * f_there) / norm

    def normalise(slot, g):
        factor = jnp.exp((peaks[slot] - peak[g]) * SCALE) / total[g]
        p = probs[slot].astype(F32) * factor
        probs[slot] = p.astype(BF16)
        gscore[slot] = (p * (gprob[slot] - centre[g]) * SCALE).astype(BF16)

    def normalise_low(i, _):
        normalise(i, i // 4)
        return 0

    def normalise_high(i, _):
        normalise(16 + i, i // 4)
        return 0

    lax.fori_loop(0, 16, normalise_low, 0)
    lax.fori_loop(0, 8, normalise_high, 0)

    def low_rows(ref, g):
        return ref[pl.ds(g * 4, 4)].reshape(1024, 512)

    def all_rows(ref, g):
        return jnp.concatenate([low_rows(ref, g), ref[pl.ds(16 + g * 4, 4)].reshape(1024, 512)], axis=0)

    def out_high(g, _):
        out_t[g] = mm(keys_t[0:512, :], all_rows(probs, g)).astype(BF16)
        return 0

    def out_lower(g, _):
        out_t[g] = mm(keys_t[0:512, 0:1024], low_rows(probs, g)).astype(BF16)
        return 0

    lax.fori_loop(0, 2, out_high, 0)
    lax.fori_loop(2, 4, out_lower, 0)

    def by_head(ref, pair_of_heads):
        lanes = pl.ds(pl.multiple_of(pair_of_heads * 128, 128), 128)
        parts = [ref[g, 0:512, lanes] for g in (2, 0, 3, 1)]
        return [jnp.concatenate([part[:, k * 64 : k * 64 + 64] for part in parts], axis=1) for k in range(2)]

    def value_terms(pair_of_heads, _):
        for k, left in enumerate(by_head(out_t, pair_of_heads)):
            lanes = pl.ds(pl.multiple_of(pair_of_heads * 256 + k * 128, 128), 128)
            right = jnp.concatenate([gout_o[:, lanes], gout_p[:, lanes]], axis=0)
            up[0, :, :, lanes] = mm(left, right).astype(BF16).reshape(4, 128, 128)
        return 0

    lax.fori_loop(0, 4, value_terms, 0)
    start("C00", "C10")

    def full_high(g, _):
        dq_t[g] = mm(keys_t[0:576, :], all_rows(gscore, g)).astype(BF16)
        return 0

    def full_lower(g, _):
        dq_t[g] = mm(keys_t[0:576, 0:1024], low_rows(gscore, g)).astype(BF16)
        return 0

    lax.fori_loop(0, 2, full_high, 0)
    lax.fori_loop(2, 4, full_lower, 0)
    start("ro1", "ro3")

    def sum_core(i):
        wait(f"C0{i}", f"C1{i}")
        uzs[i] = (up[i, f2].astype(F32) + uc[i, 1].astype(F32)).astype(BF16)
        start(f"Z{i}")

    sum_core(0)

    def key_terms(pair_of_heads, _):
        for k, left in enumerate(by_head(dq_t, pair_of_heads)):
            lanes = pl.ds(pl.multiple_of(pair_of_heads * 256 + k * 128, 128), 128)
            right = jnp.concatenate([nope_o[:, lanes], nope_p[:, lanes]], axis=0)
            up[1, :, :, lanes] = mm(left, right).astype(BF16).reshape(4, 128, 128)
            back = mm(wk_t[lanes, :], left)
            gn_own[lanes, :] = back[:, 0:128]
            gn_send[lanes, :] = back[:, 128:256].astype(BF16)
        return 0

    lax.fori_loop(0, 4, key_terms, 0)
    start("C01", "C11", "gn")

    def sum_far(i):
        wait(f"Z{i}")
        whole = up[i, f].astype(F32) + uc[i, 0].astype(F32) + uz[i].astype(F32)
        us1[i] = whole.astype(BF16).reshape(4, 2, 16, 1024)
        start(f"P{i}")

    def sum_pair(i):
        wait(f"P{i}")
        us2[i] = (us1[i, :, zl].astype(F32) + upr[i].astype(F32)).astype(BF16)
        start(f"Yp{i}", f"Ym{i}", f"Y2{i}")

    def sum_y(i):
        wait(f"Yp{i}", f"Ym{i}", f"Y2{i}")
        whole = us2[i, y].astype(F32) + uyr[i, 0].astype(F32) + uyr[i, 1].astype(F32) + uyr[i, 2].astype(F32)
        us3[i] = whole.astype(BF16)
        start(f"Xp{i}", f"Xm{i}", f"X2{i}")

    def sum_x(i, lanes):
        wait(f"Xp{i}", f"Xm{i}", f"X2{i}")
        whole = us3[i].astype(F32) + uxr[i, 0].astype(F32) + uxr[i, 1].astype(F32) + uxr[i, 2].astype(F32)
        mine_rows = whole[0:4]
        for xx in range(1, 4):
            mine_rows = jnp.where(x == xx, whole[xx * 4 : xx * 4 + 4], mine_rows)
        gu_out[:, lanes] = mine_rows

    def b_second(i):
        wait(f"B1{i}")
        add_into(dkb.at[turns[i], xp if i % 2 == 0 else xm, pl.ds(80, 64)], rb1.at[i])
        start(f"B2p{i}", f"B2m{i}")

    def b_last(i):
        wait(f"B2p{i}", f"B2m{i}")
        add_into(dkb.at[turns[i], x, pl.ds(80, 64)], rb2.at[i, 0], rb2.at[i, 1])

    def key_turn(i, _):
        t = (y + jnp.where(i == 0, 2, jnp.where(i == 1, 1, jnp.where(i == 2, 3, 0)))) % 4
        low = mm(gscore[t], query[0]) + mm(gscore[4 + t], query[1]) + mm(gscore[8 + t], query[2]) + mm(gscore[12 + t], query[3])
        low_value = mm(probs[t], grad[0]) + mm(probs[4 + t], grad[1]) + mm(probs[8 + t], grad[2]) + mm(probs[12 + t], grad[3])
        dkb[t, :, 0:64] = (low[:, 0:512] + low_value).astype(BF16).reshape(4, 64, 512)
        high = mm(gscore[16 + t], query[0]) + mm(gscore[20 + t], query[1])
        high_value = mm(probs[16 + t], grad[0]) + mm(probs[20 + t], grad[1])
        dkb[t, :, 80:144] = (high[:, 0:512] + high_value).astype(BF16).reshape(4, 64, 512)
        for xx in range(4):
            rows = [half[xx * 64 + s * 16 : xx * 64 + s * 16 + 16, 512:576] for half in (low, high) for s in range(4)]
            dkb[t, xx, 64:80] = jnp.concatenate(rows, axis=1).astype(BF16)

        @pl.when(i == 0)
        def _():
            start("A1p", "A1m", "B10")
            sum_core(1)

        @pl.when(i == 1)
        def _():
            wait("A1p")
            add_into(dkb.at[yp, pl.ds(0, 2), pl.ds(0, 80)], ra1.at[0])
            start("A2p", "B11")
            b_second(0)

        @pl.when(i == 2)
        def _():
            wait("A1m")
            add_into(dkb.at[ym, pl.ds(2, 2), pl.ds(0, 80)], ra1.at[1])
            start("A2m", "B12")
            b_second(1)
            b_last(0)
            start("B3p", "B3m")
            sum_far(0)

        @pl.when(i == 3)
        def _():
            start("B13")
            wait("A2p", "A2m")
            add_into(dkb.at[y, :, pl.ds(0, 80)], ra2.at[0], ra2.at[1])
            start("A3p", "A3m")
            b_second(2)
            b_last(1)
            wait("B3p")
            add_into(dkb.at[yp, x, pl.ds(80, 32)], rb3.at[0])
            start("B4p")
            b_second(3)

        return 0

    lax.fori_loop(0, 4, key_turn, 0)
    sum_pair(0)
    b_last(2)
    wait("B3m")
    add_into(dkb.at[ym, x, pl.ds(112, 32)], rb3.at[1])
    start("B4m")
    wait("A3p")
    add_into(dkb.at[y, xp, pl.ds(0, 48)], ra3.at[pl.ds(0, 48)])
    start("A4p")
    wait("A3m")
    add_into(dkb.at[y, xm, pl.ds(48, 32)], ra3.at[pl.ds(48, 32)])
    start("A4m")
    sum_far(1)
    sum_y(0)

    wait("gn", "ro1", "ro3")
    gn_out[...] = jnp.transpose(gn_own[...] + gn_recv[...].astype(F32)).astype(BF16)
    for half, g, slot in ((0, 2, 1), (1, 0, 0)):
        rope = dq_t[g, 512:576].astype(F32) + ro_recv[slot].astype(F32)
        rope = jnp.transpose(rope)
        gr_out[half * 64 : half * 64 + 64, :] = jnp.concatenate(
            [rope[h * 64 : h * 64 + 64] for h in range(HEADS)], axis=1
        ).astype(BF16)

    sum_pair(1)
    b_last(3)
    wait("A4p", "A4m")
    upper = dkb[y, x, 0:80].astype(F32) + ra4[0].astype(F32) + ra4[1].astype(F32)
    gl_out[0:64, 0:512] = upper[0:64].astype(BF16)
    for s in range(8):
        gl_out[s * 16 : s * 16 + 16, 512:576] = upper[64:80, s * 64 : s * 64 + 64].astype(BF16)
    wait("B4p", "B4m")
    lower = dkb[y, x, 80:144].astype(F32) + rb4[0].astype(F32) + rb4[1].astype(F32)
    gl_out[64:128, 0:512] = lower.astype(BF16)
    sum_y(1)
    sum_x(0, slice(1024, 2048))
    sum_x(1, slice(0, 1024))
    for name in made:
        made[name]().wait_send()


def per_device(query_nope, query_rope, latent, grad_out, w_up, block_order):
    shapes = [
        ((16, 144, 512), BF16), ((8, 256, 640), BF16), ((640, 2048), BF16),
        ((128, 1024), BF16), ((128, 512), BF16), ((128, 1024), BF16), ((4, 128, 2048), BF16), ((1024, 512), BF16),
        ((4, 512, 640), BF16), ((4, 512, 512), BF16), ((24, 256, 512), BF16), ((24, 256, 512), F32), ((24, 256, 512), BF16),
        ((24, 1, 512), F32), ((4, 1, 512), F32), ((4, 1, 512), F32), ((4, 1, 512), F32), ((4, 8, 512), F32), ((4, 8, 512), F32),
        ((4, 576, 512), BF16), ((4, 512, 512), BF16), ((1024, 128), F32), ((1024, 128), BF16), ((1024, 128), BF16), ((2, 64, 512), BF16),
        ((4, 4, 144, 512), BF16), ((2, 2, 80, 512), BF16), ((2, 4, 80, 512), BF16), ((80, 512), BF16), ((2, 80, 512), BF16),
        ((4, 64, 512), BF16), ((4, 2, 64, 512), BF16), ((2, 32, 512), BF16), ((2, 64, 512), BF16),
        ((2, 4, 128, 1024), BF16), ((2, 2, 128, 1024), BF16), ((2, 128, 1024), BF16), ((2, 128, 1024), BF16),
        ((2, 4, 2, 16, 1024), BF16), ((2, 4, 16, 1024), BF16), ((2, 4, 16, 1024), BF16), ((2, 3, 16, 1024), BF16),
        ((2, 16, 1024), BF16), ((2, 3, 16, 1024), BF16),
    ]
    vmem = pl.BlockSpec(memory_space=pltpu.VMEM)
    gn, gr, gl, gu = pl.pallas_call(
        kernel,
        out_shape=(
            jax.ShapeDtypeStruct((128, 1024), BF16),
            jax.ShapeDtypeStruct((128, 512), BF16),
            jax.ShapeDtypeStruct((128, 576), BF16),
            jax.ShapeDtypeStruct((4, 2048), F32),
        ),
        in_specs=[pl.BlockSpec(memory_space=pltpu.SMEM)] + [vmem] * 5,
        out_specs=(vmem,) * 4,
        scratch_shapes=[pltpu.VMEM(shape, dtype) for shape, dtype in shapes]
        + [pltpu.SemaphoreType.DMA((COPIES,)), pltpu.SemaphoreType.DMA((COPIES,))],
        compiler_params=pltpu.CompilerParams(
            collective_id=0, has_side_effects=True, vmem_limit_bytes=63 * 1024 * 1024
        ),
        name="latent_attention_backward",
    )(block_order, latent[0], query_nope[0], query_rope[0], grad_out[0], w_up)
    return gn[None], gr[None], gl[None], gu


def solution(mesh):
    rows = P("fsdp", "blk", None)
    return jax.shard_map(
        per_device,
        mesh=mesh,
        in_specs=(rows, rows, rows, rows, P("fsdp", None), P()),
        out_specs=(rows, rows, rows, P(("fsdp", "blk"), None)),
        check_vma=False,
    )
```

time: 1290 us -> 111 us (0.09)
  waiting for transfers between devices: 527 us -> 0 us
  matrix products: 314 us -> 0 us
  local copies, waits for them, and re-layouts: 306 us -> 7.19 us
  Pallas kernels: 0 us -> 103 us
  loops' own time: 92.5 us -> 0 us
  other arithmetic: 24.5 us -> 0 us
  between operations: 14.7 us -> 0.66 us
    ppermute x94 -> x0, waiting for transfers between devices: 363 us -> none  [from_behind(): return lax.ppermute(block, axis, route)]
    dot_general x519 -> x0, matrix products: 314 us -> none  [the longest x65 123 us: backward_visit(): jnp.einsum('htu,thk->uk', grad_low, query_rows, preferred_element_type=jn...]
    dynamic_slice x315 -> x0, local copies, waits for them, and re-layouts: 165 us -> none  [the longest x62 56.9 us: source_of(): lax.dynamic_index_in_dim(first_blocks, source, 0, keepdims=False)]
    unnamed x3 -> x0, waiting for transfers between devices: 140 us -> none
    while x283 -> x0, local copies, waits for them, and re-layouts: 108 us -> none
    pallas_call x0 -> x1, Pallas kernels: none -> 103 us  [per_device(): pl.pallas_call(kernel, out_shape=(jax.ShapeDtypeStruct((128, 1024), BF16)...]
    another operation x2 -> x0, loops' own time: 92.5 us -> none  [the longest x1 47.7 us: per_device(): lax.fori_loop(1, blocks, backward_turn, (own_keys, carry))[1]]
    all_gather x1 -> x0, waiting for transfers between devices: 25.2 us -> none  [per_device(): weights = lax.all_gather(w_up, 'fsdp', axis=0, tiled=True)]
  transfers between devices with their start and end apart: 96 -> 0, of which waited for: 67 -> 0; matrix products, arithmetic and copies ran while one was open for 23% -> 0% of each run, Pallas kernels for 0% -> 0%
where the time goes in v1:
time: 111 us
  Pallas kernels  103 us (93%)
  local copies, waits for them, and re-layouts  7.19 us (6%)
    pallas_call x1, Pallas kernels, per_device(): pl.pallas_call(kernel, out_shape=(jax.ShapeDtypeStruct((128, 1024), BF16)...  103 us
    unnamed x14, local copies, waits for them, and re-layouts  7.19 us

profile of v1, /device:TPU:0, one launch (start us, length us, event | category | flops | bytes accessed | tf_op | source)
XLA Modules:
  0.0 110.8 jit_solution(9852141124429813718)
XLA Ops:
  0.6 0.0 copy-start.3
  0.6 0.7 copy-done.3
  1.3 0.7 copy.11.order
  2.0 1.7 %copy.10 = bf16[1,128,576]{2,1,0:T(8,128)(2,1)} copy(bf16[1,128,576]{1,2,0:T(8,128)(2,1)} %param.8) | data formatting | bytes 294912 | tf_op args[2]
  3.7 103.0 %latent_attention_backward.1 = (bf16[128,1024]{1,0:T(8,128)(2,1)}, bf16[128,512]{1,0:T(8,128)(2,1)}, bf16[128,576]{1,0:T(8,128)(2,1)}, f32[4,2048]{1,0:T(4,128)}) custom-call(s32[32,2]{1,0:T(8,128)} %copy.11.order, bf16[128,576]{1,0:T(8,128)(2,1)} %bitcast.7, bf16[128,1024]{1,0:T(8,128)(2,1)} %bitcast.9, bf16[128,512]{1,0:T(8,128)(2,1)} %bitcast.13, ...), custom_call_target="tpu_custom_call" | custom-call | tf_op jit(solution)/shard_map/latent_attention_backward/pallas_call | solution.py:543
  106.7 0.0 copy-start
  106.7 1.7 %copy.12 = bf16[1,128,576]{1,2,0:T(8,128)(2,1)} copy(bf16[1,128,576]{2,1,0:T(8,128)(2,1)} %bitcast.11) | data formatting | bytes 294912
  108.4 0.0 copy-done
  108.5 0.0 copy-start.1
  108.5 0.7 copy.16
  109.2 0.3 copy-done.1
  109.5 0.0 copy-start.2
  109.5 0.7 copy.17
  110.1 0.1 copy-done.2
  110.2 0.6 copy.18
Async XLA Ops:
  0.6 0.7 copy-start.3
  106.7 1.8 %copy-start = (bf16[128,1024]{1,0:T(8,128)(2,1)S(1)}, bf16[128,1024]{1,0:T(8,128)(2,1)}, u32[]{:S(2)}) copy-start(bf16[128,1024]{1,0:T(8,128)(2,1)} %get-tuple-element.8) | copy-start | bytes 786436
  108.5 1.0 copy-start.1
  109.5 0.8 copy-start.2

commit v2 on v1

v2 whole, which is shorter than its diff:
```python
import functools
import math

import jax
import jax.numpy as jnp
from jax import lax
from jax.experimental import pallas as pl
from jax.experimental.pallas import tpu as pltpu
from jax.sharding import PartitionSpec as P

HEADS = 8
LATENT = 512
SCALE = 1.0 / math.sqrt(192.0)
NEG_FILL = -1e30
F32 = jnp.float32
BF16 = jnp.bfloat16
MESH = pl.DeviceIdType.MESH
COPIES = 112


def mm(a, b):
    return lax.dot_general(a, b, (((1,), (0,)), ((), ())), preferred_element_type=F32)


def mm_nt(a, b):
    return lax.dot_general(a, b, (((1,), (1,)), ((), ())), preferred_element_type=F32)


def add_into(ref, *others):
    total = ref[...].astype(F32)
    for other in others:
        total = total + other[...].astype(F32)
    ref[...] = total.astype(BF16)


def kernel(
    order, lat, nope_o, rope_o, gout_o, w_own,
    gn_out, gr_out, gl_out, gu_out,
    kbuf, keys, keys_t, nope_p, rope_p, gout_p, w_all, wk_t,
    query, grad, probs, gprob, gscore, peaks, peak, total, centre, stat_s, stat_r,
    dq_t, out_t, gn_own, gn_send, gn_recv, ro_recv,
    dkb, ra1, ra2, ra3, rb1, rb2, rb3,
    up, uc, uzs, uz, us2, uyr, us3, uxr,
    send, recv,
):
    f = lax.axis_index("fsdp")
    blk = lax.axis_index("blk")
    x, zl, y = blk % 4, (blk // 4) % 2, blk // 8
    xp, xm, x2 = (x + 1) % 4, (x + 3) % 4, (x + 2) % 4
    yp, ym, y2 = (y + 1) % 4, (y + 3) % 4, (y + 2) % 4
    f1 = f + 1 - 2 * (f % 2)
    f2 = (f + 2) % 4
    f3 = (f1 + 2) % 4
    pair_blk = blk + 4 - 8 * zl

    def at(yy, xx):
        return {"blk": (yy * 2 + zl) * 4 + xx}

    to_xp, to_xm, to_x2 = at(y, xp), at(y, xm), at(y, x2)
    to_yp, to_ym, to_y2 = at(yp, x), at(ym, x), at(y2, x)
    to_pair = {"blk": pair_blk}
    to_core = {"fsdp": f1}
    to_far = {"fsdp": f2, "blk": pair_blk}
    to_z2 = {"fsdp": f2}

    made = {}

    def define(name, src, dst, device):
        number = len(made)
        made[name] = lambda: pltpu.make_async_remote_copy(
            src_ref=src(), dst_ref=dst(), send_sem=send.at[number], recv_sem=recv.at[number],
            device_id=device, device_id_type=MESH,
        )

    def start(*names):
        for name in names:
            made[name]().start()

    def wait(*names):
        for name in names:
            made[name]().wait_recv()

    def same(name, part, device):
        define(name, part, part, device)

    for name, first, swap in (("a", 0, False), ("b", 288, True)):
        def part(dy, dx, first=first, swap=swap):
            if swap:
                dy, dx = dx, dy
            return lambda: kbuf.at[((y + dy) % 4) * 4 + (x + dx) % 4, pl.ds(first, 288)]

        if swap:
            ip, im, i2, jp, jm = to_yp, to_ym, to_y2, to_xp, to_xm
        else:
            ip, im, i2, jp, jm = to_xp, to_xm, to_x2, to_yp, to_ym
        same(name + "1", part(0, 0), ip)
        same(name + "2", part(0, 0), im)
        same(name + "5", part(0, 0), i2)
        same(name + "3", part(0, 0), jp)
        same(name + "4", part(0, 0), jm)
        same(name + "7", part(0, 3), jp)
        same(name + "8", part(0, 3), jm)
        same(name + "9", part(0, 1), jp)
        same(name + "10", part(0, 1), jm)
        same(name + "11", part(0, 2), jp)
        same(name + "12", part(0, 2), jm)
        same(name + "13", part(3, 0), jp)
        same(name + "14", part(3, 3), jp)
        same(name + "15", part(1, 1), jm)
        same(name + "16", part(1, 2), jm)

    define("qn", lambda: nope_o, lambda: nope_p, to_pair)
    define("qr", lambda: rope_o, lambda: rope_p, to_pair)
    define("qg", lambda: gout_o, lambda: gout_p, to_pair)
    for name, first in (("k", 0), ("v", 1024)):
        def own_w(first=first):
            return w_own.at[:, pl.ds(first, 1024)]

        def far_w(shard, first=first):
            return lambda: w_all.at[shard, :, pl.ds(first, 1024)]

        define(f"w{name}1", own_w, far_w(f), to_core)
        define(f"w{name}2", own_w, far_w(f), to_far)
        define(f"w{name}3", far_w(f2), far_w(f2), to_core)
    define("st0", lambda: stat_s.at[pl.ds(0, 2)], lambda: stat_r.at[pl.ds(2, 2)], to_pair)
    define("st1", lambda: stat_s.at[pl.ds(2, 2)], lambda: stat_r.at[pl.ds(0, 2)], to_pair)
    define("gn", lambda: gn_send, lambda: gn_recv, to_pair)
    define("ro0", lambda: dq_t.at[2, pl.ds(512, 64)], lambda: ro_recv.at[0], to_pair)
    define("ro1", lambda: dq_t.at[3, pl.ds(512, 64)], lambda: ro_recv.at[1], to_pair)

    def term(yy, xx, first):
        return lambda: dkb.at[yy, xx, pl.ds(first, 288)]

    def term_rows(yy, x_first, x_count):
        return lambda: dkb.at[yy, pl.ds(x_first, x_count), pl.ds(0, 288)]

    define("A1p", term_rows(y2, 0, 2), lambda: ra1.at[0], to_yp)
    define("A1m", term_rows(y2, 2, 2), lambda: ra1.at[1], to_ym)
    define("A2p", term_rows(yp, 0, 4), lambda: ra2.at[0], to_yp)
    define("A2m", term_rows(ym, 0, 4), lambda: ra2.at[1], to_ym)
    define("A3p", term(y, xp, 0), lambda: ra3.at[0], to_xp)
    define("A3m", term(y, xm, 0), lambda: ra3.at[1], to_xm)
    define("A32", term(y, x2, 0), lambda: ra3.at[2], to_x2)
    turns = (y2, yp, ym, y)
    for i in range(4):
        to_first = to_x2 if i == 3 else (to_xp if i % 2 == 0 else to_xm)
        define(f"B1{i}", term(turns[i], x2, 288), lambda i=i: rb1.at[i], to_first)
        define(f"B2p{i}", term(turns[i], xp, 288), lambda i=i: rb2.at[i, 0], to_xp)
        define(f"B2m{i}", term(turns[i], xm, 288), lambda i=i: rb2.at[i, 1], to_xm)
    for i, device in enumerate((to_y2, to_yp, to_ym)):
        define(f"B3{i}", term(turns[i], x, 288), lambda i=i: rb3.at[i], device)

    for i in range(2):
        define(f"C0{i}", lambda i=i: up.at[i, f1], lambda i=i: uc.at[i, 0], to_core)
        define(f"C1{i}", lambda i=i: up.at[i, f3], lambda i=i: uc.at[i, 1], to_core)
        for j, device in enumerate((to_pair, to_far, to_z2)):
            define(f"Z{j}{i}", lambda i=i, j=j: uzs.at[i, j], lambda i=i, j=j: uz.at[i, j], device)
        for j, (yy, device) in enumerate(((yp, to_yp), (ym, to_ym), (y2, to_y2))):
            define(f"Y{j}{i}", lambda i=i, yy=yy: us2.at[i, yy], lambda i=i, j=j: uyr.at[i, j], device)
        for j, device in enumerate((to_xp, to_xm, to_x2)):
            define(f"X{j}{i}", lambda i=i: us3.at[i], lambda i=i, j=j: uxr.at[i, j], device)

    kbuf[y * 4 + x] = lat[...]
    barrier = pltpu.get_barrier_semaphore()
    partners = (to_xp, to_xm, to_x2, to_yp, to_ym, to_y2, to_pair, to_core, to_far, to_z2)
    for partner in partners:
        pl.semaphore_signal(barrier, inc=1, device_id=partner, device_id_type=MESH)
    pl.semaphore_wait(barrier, len(partners))

    start("wk2", "qn", "a1", "b1", "a2", "b2", "a5", "b5", "a3", "b3", "a4", "b4", "qr", "wk1")
    w_all[f] = w_own[...]
    query[:, 512:640, :] = jnp.zeros((4, 128, 512), BF16)
    keys[:, :, 512:640] = jnp.zeros((8, 256, 128), BF16)

    def place_rope(rope, s):
        for k in range(4):
            turned = jnp.transpose(rope[:, k * 128 : k * 128 + 128].astype(F32))
            lanes = slice(k * 128, k * 128 + 128)
            query[2 * s + 1, 512:576, lanes] = jnp.concatenate([turned[:64, :64], turned[64:, :64]], axis=1).astype(BF16)
            query[2 * s, 512:576, lanes] = jnp.concatenate([turned[:64, 64:], turned[64:, 64:]], axis=1).astype(BF16)

    place_rope(rope_o, 0)
    for name in ("a", "b"):
        wait(name + "1")
        start(name + "7", name + "8")
    for name in ("a", "b"):
        wait(name + "2")
        start(name + "9", name + "10")
    for name in ("a", "b"):
        wait(name + "5")
        start(name + "11", name + "12")
    start("wv2", "qg", "wv1")
    for name in ("a", "b"):
        wait(name + "3")
        start(name + "13")
    wait("wk2")
    start("wk3")
    for name in ("a", "b"):
        wait(name + "7")
        start(name + "14")
    for name in ("a", "b"):
        wait(name + "10")
        start(name + "15")
    for name in ("a", "b"):
        wait(name + "12")
        start(name + "16")

    def blocks(value, lanes):
        both = value[:, lanes]
        empty = jnp.zeros((64, 128), BF16)
        rows = []
        for half in (both[:64], both[64:]):
            rows.append(jnp.concatenate([half[:, :128], empty], axis=1))
            rows.append(jnp.concatenate([empty, half[:, 128:]], axis=1))
        return jnp.concatenate(rows, axis=0)

    def project(value, first, ref, s):
        def two_heads(k, _):
            lanes = pl.ds(pl.multiple_of(k * 256, 256), 256)
            w_lanes = pl.ds(pl.multiple_of(first + k * 256, 256), 256)
            to = pl.ds(pl.multiple_of(k * 128, 128), 128)
            out = mm_nt(w_all[:, :, w_lanes].reshape(512, 256), blocks(value, lanes)).astype(BF16)
            ref[2 * s + 1, 0:512, to] = out[:, :128]
            ref[2 * s, 0:512, to] = out[:, 128:]
            return 0

        lax.fori_loop(0, 4, two_heads, 0)

    wait("wk1", "wk3")
    project(nope_o, 0, query, 0)
    for s in range(4):
        wk_t[:, s * 128 : s * 128 + 128] = jnp.transpose(w_all[s, :, 0:1024])
    wait("qn", "qr")
    place_rope(rope_p, 1)
    project(nope_p, 0, query, 1)

    for name in ("a", "b"):
        wait(*(name + n for n in ("4", "8", "9", "11", "13", "14", "15", "16")))

    def assemble(i, _):
        yy, xx = i // 2, (i % 2) * 2
        both = [kbuf[yy * 4 + xx + j] for j in range(2)]
        lanes = pl.ds(pl.multiple_of(i * 128, 128), 128)
        high_lanes = pl.ds(pl.multiple_of(1024 + i * 128, 128), 128)
        keys_t[:, lanes] = jnp.concatenate([b[:, :64] for b in both], axis=1)
        keys_t[:, high_lanes] = jnp.concatenate([b[:, 64:] for b in both], axis=1)
        for j in range(2):
            rows = pl.ds(pl.multiple_of((xx + j) * 64, 64), 64)
            main = jnp.transpose(both[j][:512])
            rest = jnp.transpose(both[j][512:])
            keys[yy, rows, 0:512] = main[:64]
            keys[yy, rows, 512:576] = rest[:64]
            keys[4 + yy, rows, 0:512] = main[64:]
            keys[4 + yy, rows, 512:576] = rest[64:]
        return 0

    lax.fori_loop(0, 8, assemble, 0)
    wait("wv2")
    start("wv3")
    wait("wv1", "wv3")
    project(gout_o, 1024, grad, 0)

    peak[...] = jnp.full((4, 1, 512), NEG_FILL, F32)
    total[...] = jnp.zeros((4, 1, 512), F32)
    centre[...] = jnp.zeros((4, 1, 512), F32)
    relative = lax.broadcasted_iota(jnp.int32, (64, 512), 0) - lax.broadcasted_iota(jnp.int32, (64, 512), 1) % 64

    def visit(t, g, high, masked, first):
        tile = 4 + t if high else t
        slot = 16 + (g // 2) * 4 + t if high else g * 4 + t
        scores = mm(keys[tile], query[g])
        grad_probs = mm(keys[tile, :, 0:512], grad[g])
        if masked:
            block = 63 - first if high else first
            parts = []
            for xx in range(4):
                key_first = order[0, (t * 2 + zl) * 4 + xx]
                key_block = 63 - key_first if high else key_first
                parts.append(relative <= (block - key_block) * 64)
            allowed = jnp.concatenate(parts, axis=0)
            scores = jnp.where(allowed, scores, NEG_FILL)
        old = peak[g]
        new = jnp.maximum(old, jnp.max(scores, axis=0, keepdims=True))
        weights = jnp.exp((scores - new) * SCALE)
        if masked:
            weights = jnp.where(allowed, weights, 0.0)
        factor = jnp.exp((old - new) * SCALE)
        total[g] = total[g] * factor + jnp.sum(weights, axis=0, keepdims=True)
        centre[g] = centre[g] * factor + jnp.sum(weights * grad_probs, axis=0, keepdims=True)
        peak[g] = new
        probs[slot] = weights.astype(BF16)
        gprob[slot] = grad_probs
        peaks[slot] = new

    def visits(s, first):
        def step(t, _):
            visit(t, 2 * s, False, False, first)
            visit(t, 2 * s + 1, False, True, first)
            visit(t, 2 * s, True, True, first)
            return 0

        lax.fori_loop(0, 4, step, 0)
        for g in (2 * s, 2 * s + 1):
            stat_s[g, 0:1] = peak[g]
            stat_s[g, 1:2] = total[g]
            stat_s[g, 2:3] = centre[g]
        start(f"st{s}")

    visits(0, order[0, blk])
    wait("qg")
    project(gout_p, 1024, grad, 1)
    visits(1, order[0, pair_blk])

    def normalise(slot, g):
        factor = jnp.exp((peaks[slot] - peak[g]) * SCALE) / total[g]
        p = probs[slot].astype(F32) * factor
        probs[slot] = p.astype(BF16)
        gscore[slot] = (p * (gprob[slot] - centre[g]) * SCALE).astype(BF16)

    def low_rows(ref, g):
        return ref[g * 4 : g * 4 + 4].reshape(1024, 512)

    def all_rows(ref, g):
        return jnp.concatenate([low_rows(ref, g), ref[16 + g * 2 : 20 + g * 2].reshape(1024, 512)], axis=0)

    def merge(s):
        wait(f"st{1 - s}")
        for g in (2 * s, 2 * s + 1):
            here, there = stat_s[g], stat_r[g]
            new = jnp.maximum(here[0:1], there[0:1])
            f_here = jnp.exp((here[0:1] - new) * SCALE)
            f_there = jnp.exp((there[0:1] - new) * SCALE)
            norm = here[1:2] * f_here + there[1:2] * f_there
            peak[g] = new
            total[g] = norm
            centre[g] = (here[2:3] * f_here + there[2:3] * f_there) / norm

        def low_slots(i, _):
            normalise(s * 8 + i, 2 * s + i // 4)
            return 0

        def high_slots(i, _):
            normalise(16 + s * 4 + i, 2 * s)
            return 0

        lax.fori_loop(0, 8, low_slots, 0)
        lax.fori_loop(0, 4, high_slots, 0)
        out_t[2 * s] = mm(keys_t[0:512, :], all_rows(probs, 2 * s)).astype(BF16)
        out_t[2 * s + 1] = mm(keys_t[0:512, 0:1024], low_rows(probs, 2 * s + 1)).astype(BF16)

    merge(1)
    merge(0)

    def two_heads_of(ref, k):
        lanes = pl.ds(pl.multiple_of(k * 128, 128), 128)
        return jnp.concatenate([ref[g, 0:512, lanes] for g in range(4)], axis=1)

    def two_heads_rows(own, pair, k):
        lanes = pl.ds(pl.multiple_of(k * 256, 256), 256)
        mine, other = blocks(own, lanes), blocks(pair, lanes)
        return jnp.concatenate([mine[128:], mine[:128], other[128:], other[:128]], axis=0)

    def value_terms(k, _):
        lanes = pl.ds(pl.multiple_of(k * 256, 256), 256)
        whole = mm(two_heads_of(out_t, k), two_heads_rows(gout_o, gout_p, k))
        up[0, :, :, lanes] = whole.astype(BF16).reshape(4, 128, 256)
        return 0

    lax.fori_loop(0, 4, value_terms, 0)
    start("C00", "C10")

    for s in (1, 0):
        dq_t[2 * s] = mm(keys_t[...], all_rows(gscore, 2 * s)).astype(BF16)
        dq_t[2 * s + 1] = mm(keys_t[:, 0:1024], low_rows(gscore, 2 * s + 1)).astype(BF16)

    def sum_core(i):
        wait(f"C0{i}", f"C1{i}")
        for j, (shard, slot, plane) in enumerate(((f, 0, 1 - zl), (f2, 1, 1 - zl), (f2, 1, zl))):
            for yy in range(4):
                rows = pl.ds(pl.multiple_of(yy * 32 + plane * 16, 16), 16)
                whole = up[i, shard, rows].astype(F32) + uc[i, slot, rows].astype(F32)
                uzs[i, j, yy] = whole.astype(BF16)
        start(f"Z0{i}", f"Z1{i}", f"Z2{i}")

    sum_core(0)

    def key_terms(k, _):
        lanes = pl.ds(pl.multiple_of(k * 256, 256), 256)
        left = two_heads_of(dq_t, k)
        whole = mm(left, two_heads_rows(nope_o, nope_p, k))
        up[1, :, :, lanes] = whole.astype(BF16).reshape(4, 128, 256)
        back = mm(wk_t[lanes, :], left)
        for j in range(2):
            rows = pl.ds(pl.multiple_of(k * 256 + j * 128, 128), 128)
            tiles = [back[j * 128 : j * 128 + 128, g * 128 + j * 64 : g * 128 + j * 64 + 64] for g in range(4)]
            gn_own[rows, :] = jnp.concatenate([tiles[1], tiles[0]], axis=1)
            gn_send[rows, :] = jnp.concatenate([tiles[3], tiles[2]], axis=1).astype(BF16)
        return 0

    lax.fori_loop(0, 4, key_terms, 0)
    start("C01", "C11")

    def sum_z(i):
        wait(f"Z0{i}", f"Z1{i}", f"Z2{i}")
        for yy in range(4):
            rows = pl.ds(pl.multiple_of(yy * 32 + zl * 16, 16), 16)
            whole = up[i, f, rows].astype(F32) + uc[i, 0, rows].astype(F32)
            for j in range(3):
                whole = whole + uz[i, j, yy].astype(F32)
            us2[i, yy] = whole.astype(BF16)
        start(f"Y0{i}", f"Y1{i}", f"Y2{i}")

    def sum_y(i):
        wait(f"Y0{i}", f"Y1{i}", f"Y2{i}")
        whole = us2[i, y].astype(F32) + uyr[i, 0].astype(F32) + uyr[i, 1].astype(F32) + uyr[i, 2].astype(F32)
        us3[i] = whole.astype(BF16)
        start(f"X0{i}", f"X1{i}", f"X2{i}")

    def sum_x(i, lanes):
        wait(f"X0{i}", f"X1{i}", f"X2{i}")
        whole = us3[i].astype(F32) + uxr[i, 0].astype(F32) + uxr[i, 1].astype(F32) + uxr[i, 2].astype(F32)
        mine_rows = whole[0:4]
        for xx in range(1, 4):
            mine_rows = jnp.where(x == xx, whole[xx * 4 : xx * 4 + 4], mine_rows)
        gu_out[:, lanes] = mine_rows

    lower = pl.ds(288, 288)

    def b_second(i):
        wait(f"B1{i}")
        add_into(dkb.at[turns[i], xp if i % 2 == 0 else xm, lower], rb1.at[i])
        start(f"B2p{i}", f"B2m{i}")

    def b_last(i):
        wait(f"B2p{i}", f"B2m{i}")
        add_into(dkb.at[turns[i], x, lower], rb2.at[i, 0], rb2.at[i, 1])
        start(f"B3{i}")

    def key_turn(i, _):
        t = (y + jnp.where(i == 0, 2, jnp.where(i == 1, 1, jnp.where(i == 2, 3, 0)))) % 4

        def one(slots):
            a = sum(mm_nt(query[g, 0:576], gscore[slot]) for g, slot in slots)
            b = sum(mm_nt(grad[g], probs[slot]) for g, slot in slots)
            return a[:512] + b, a[512:]

        low, low_rest = one([(g, g * 4 + t) for g in range(4)])
        high, high_rest = one([(2 * s, 16 + s * 4 + t) for s in range(2)])
        for xx in range(4):
            lanes = slice(xx * 64, xx * 64 + 64)
            dkb[t, xx, 0:512] = jnp.concatenate([low[:, lanes], high[:, lanes]], axis=1).astype(BF16)
            dkb[t, xx, 512:576] = jnp.concatenate([low_rest[:, lanes], high_rest[:, lanes]], axis=1).astype(BF16)

        @pl.when(i == 0)
        def _():
            start("A1p", "A1m", "B10")
            sum_core(1)
            start("ro0", "ro1", "gn")

        @pl.when(i == 1)
        def _():
            start("B11")
            wait("A1p")
            add_into(dkb.at[yp, pl.ds(0, 2), pl.ds(0, 288)], ra1.at[0])
            start("A2p")
            b_second(0)

        @pl.when(i == 2)
        def _():
            start("B12")
            wait("A1m")
            add_into(dkb.at[ym, pl.ds(2, 2), pl.ds(0, 288)], ra1.at[1])
            start("A2m")
            b_second(1)
            b_last(0)
            sum_z(0)

        @pl.when(i == 3)
        def _():
            start("B13", "B2p3", "B2m3")
            wait("A2p", "A2m")
            add_into(dkb.at[y, :, pl.ds(0, 288)], ra2.at[0], ra2.at[1])
            start("A3p", "A3m", "A32")
            b_second(2)
            b_last(1)
            sum_z(1)
            sum_y(0)

        return 0

    lax.fori_loop(0, 4, key_turn, 0)
    b_last(2)
    sum_y(1)

    wait("gn", "ro0", "ro1")
    gn_out[...] = jnp.transpose(gn_own[...] + gn_recv[...].astype(F32)).astype(BF16)
    for half, g in ((0, 1), (1, 0)):
        rope = jnp.transpose(dq_t[g, 512:576].astype(F32) + ro_recv[g].astype(F32))
        gr_out[half * 64 : half * 64 + 64, :] = jnp.concatenate(
            [rope[h * 64 : h * 64 + 64] for h in range(HEADS)], axis=1
        ).astype(BF16)

    wait("A3p", "A3m", "A32")
    add_into(dkb.at[y, x, pl.ds(0, 288)], ra3.at[0], ra3.at[1], ra3.at[2])
    wait("B13", "B2p3", "B2m3", "B30", "B31", "B32")
    add_into(dkb.at[y, x, lower], rb1.at[3], rb2.at[3, 0], rb2.at[3, 1], rb3.at[0], rb3.at[1], rb3.at[2])
    gl_out[...] = dkb[y, x]
    sum_x(0, slice(1024, 2048))
    sum_x(1, slice(0, 1024))
    for name in made:
        made[name]().wait_send()


def per_device(query_nope, query_rope, latent, grad_out, w_up, block_order):
    shapes = [
        ((16, 576, 128), BF16), ((8, 256, 640), BF16), ((576, 2048), BF16),
        ((128, 1024), BF16), ((128, 512), BF16), ((128, 1024), BF16), ((4, 128, 2048), BF16), ((1024, 512), BF16),
        ((4, 640, 512), BF16), ((4, 512, 512), BF16), ((24, 256, 512), BF16), ((24, 256, 512), F32), ((24, 256, 512), BF16),
        ((24, 1, 512), F32), ((4, 1, 512), F32), ((4, 1, 512), F32), ((4, 1, 512), F32), ((4, 8, 512), F32), ((4, 8, 512), F32),
        ((4, 576, 512), BF16), ((4, 512, 512), BF16), ((1024, 128), F32), ((1024, 128), BF16), ((1024, 128), BF16), ((2, 64, 512), BF16),
        ((4, 4, 576, 128), BF16), ((2, 2, 288, 128), BF16), ((2, 4, 288, 128), BF16), ((3, 288, 128), BF16),
        ((4, 288, 128), BF16), ((4, 2, 288, 128), BF16), ((3, 288, 128), BF16),
        ((2, 4, 128, 1024), BF16), ((2, 2, 128, 1024), BF16), ((2, 3, 4, 16, 1024), BF16), ((2, 3, 4, 16, 1024), BF16),
        ((2, 4, 16, 1024), BF16), ((2, 3, 16, 1024), BF16), ((2, 16, 1024), BF16), ((2, 3, 16, 1024), BF16),
    ]
    vmem = pl.BlockSpec(memory_space=pltpu.VMEM)
    gn, gr, gl, gu = pl.pallas_call(
        kernel,
        out_shape=(
            jax.ShapeDtypeStruct((128, 1024), BF16),
            jax.ShapeDtypeStruct((128, 512), BF16),
            jax.ShapeDtypeStruct((576, 128), BF16),
            jax.ShapeDtypeStruct((4, 2048), F32),
        ),
        in_specs=[pl.BlockSpec(memory_space=pltpu.SMEM)] + [vmem] * 5,
        out_specs=(vmem,) * 4,
        scratch_shapes=[pltpu.VMEM(shape, dtype) for shape, dtype in shapes]
        + [pltpu.SemaphoreType.DMA((COPIES,)), pltpu.SemaphoreType.DMA((COPIES,))],
        compiler_params=pltpu.CompilerParams(
            collective_id=0, has_side_effects=True, vmem_limit_bytes=63 * 1024 * 1024
        ),
        name="latent_attention_backward",
    )(block_order.T, latent[0].T, query_nope[0], query_rope[0], grad_out[0], w_up)
    return gn[None], gr[None], gl.T[None], gu


def solution(mesh):
    rows = P("fsdp", "blk", None)
    return jax.shard_map(
        per_device,
        mesh=mesh,
        in_specs=(rows, rows, rows, rows, P("fsdp", None), P()),
        out_specs=(rows, rows, rows, P(("fsdp", "blk"), None)),
        check_vma=False,
    )
```

time: 111 us -> 92.3 us (0.83)
  Pallas kernels: 103 us -> 86.7 us
  local copies, waits for them, and re-layouts: 7.19 us -> 4.04 us
    pallas_call x1, Pallas kernels: 103 us -> 86.7 us  [per_device(): pl.pallas_call(kernel, out_shape=(jax.ShapeDtypeStruct((128, 1024), BF16)...]
    unnamed x14 -> x10, local copies, waits for them, and re-layouts: 7.19 us -> 4.04 us
where the time goes in v2:
time: 92.3 us; the launch traced here: 91.4 us
  Pallas kernels  86.7 us (94%)
  local copies, waits for them, and re-layouts  4.04 us (4%)
    pallas_call x1, Pallas kernels, per_device(): pl.pallas_call(kernel, out_shape=(jax.ShapeDtypeStruct((128, 1024), BF16)...  86.7 us
    unnamed x10, local copies, waits for them, and re-layouts  4.04 us

profile of v2, /device:TPU:0, one launch (start us, length us, event | category | flops | bytes accessed | tf_op | source)
XLA Modules:
  0.0 91.4 jit_solution(9773227867847040448)
XLA Ops:
  0.6 86.7 %latent_attention_backward.1 = (bf16[128,1024]{1,0:T(8,128)(2,1)}, bf16[128,512]{1,0:T(8,128)(2,1)}, bf16[576,128]{1,0:T(8,128)(2,1)}, f32[4,2048]{1,0:T(4,128)}) custom-call(s32[2,32]{1,0:T(2,128)} %bitcast.19, bf16[576,128]{1,0:T(8,128)(2,1)} %bitcast.15, bf16[128,1024]{1,0:T(8,128)(2,1)} %bitcast.13, bf16[128,512]{1,0:T(8,128)(2,1)} %bitcast.17, ...), custom_call_target="tpu_custom_call" | custom-call | tf_op jit(solution)/shard_map/latent_attention_backward/pallas_call | solution.py:527
  87.4 0.0 copy-start.1
  87.4 1.7 %copy.14 = bf16[1,128,1024]{2,1,0:T(8,128)(2,1)} copy(bf16[1,128,1024]{2,1,0:T(8,128)(2,1)} %bitcast.12) | data formatting | bytes 524288
  89.1 0.0 copy-done.1
  89.1 0.0 copy-start
  89.1 0.7 copy.15
  89.7 0.3 copy-done
  90.0 0.0 copy-start.2
  90.0 0.7 copy.16
  90.7 0.1 copy-done.2
  90.8 0.6 copy.17
Async XLA Ops:
  87.4 1.7 %copy-start.1 = (bf16[128,512]{1,0:T(8,128)(2,1)S(1)}, bf16[128,512]{1,0:T(8,128)(2,1)}, u32[]{:S(2)}) copy-start(bf16[128,512]{1,0:T(8,128)(2,1)} %get-tuple-element.9) | copy-start | bytes 393220
  89.1 1.0 %copy-start = (bf16[576,128]{1,0:T(8,128)(2,1)S(1)}, bf16[576,128]{1,0:T(8,128)(2,1)}, u32[]{:S(2)}) copy-start(bf16[576,128]{1,0:T(8,128)(2,1)} %get-tuple-element.10) | copy-start | bytes 442372
  90.0 0.8 copy-start.2

commit v3 on v2

--- a/solution.py
+++ b/solution.py
@@ -12,10 +12,12 @@
 LATENT = 512
 SCALE = 1.0 / math.sqrt(192.0)
 NEG_FILL = -1e30
+NEG_START = -1e20
+BASE2 = SCALE * math.log2(math.e)
 F32 = jnp.float32
 BF16 = jnp.bfloat16
 MESH = pl.DeviceIdType.MESH
-COPIES = 112
+COPIES = 144
 
 
 def mm(a, b):
@@ -34,13 +36,14 @@
 
 
 def kernel(
-    order, lat, nope_o, rope_o, gout_o, w_own,
+    order, lat_in, nope_in, rope_in, gout_in, w_in,
     gn_out, gr_out, gl_out, gu_out,
     kbuf, keys, keys_t, nope_p, rope_p, gout_p, w_all, wk_t,
     query, grad, probs, gprob, gscore, peaks, peak, total, centre, stat_s, stat_r,
     dq_t, out_t, gn_own, gn_send, gn_recv, ro_recv,
     dkb, ra1, ra2, ra3, rb1, rb2, rb3,
     up, uc, uzs, uz, us2, uyr, us3, uxr,
+    lat, nope_o, rope_o, gout_o, w_own, loads,
     send, recv,
 ):
     f = lax.axis_index("fsdp")
@@ -131,16 +134,16 @@
     def term(yy, xx, first):
         return lambda: dkb.at[yy, xx, pl.ds(first, 288)]
 
-    def term_rows(yy, x_first, x_count):
-        return lambda: dkb.at[yy, pl.ds(x_first, x_count), pl.ds(0, 288)]
-
-    define("A1p", term_rows(y2, 0, 2), lambda: ra1.at[0], to_yp)
-    define("A1m", term_rows(y2, 2, 2), lambda: ra1.at[1], to_ym)
-    define("A2p", term_rows(yp, 0, 4), lambda: ra2.at[0], to_yp)
-    define("A2m", term_rows(ym, 0, 4), lambda: ra2.at[1], to_ym)
-    define("A3p", term(y, xp, 0), lambda: ra3.at[0], to_xp)
-    define("A3m", term(y, xm, 0), lambda: ra3.at[1], to_xm)
-    define("A32", term(y, x2, 0), lambda: ra3.at[2], to_x2)
+    def column(d):
+        return (x + d) % 4
+
+    for d in range(4):
+        sign, device = ("p", to_yp) if d in (1, 2) else ("m", to_ym)
+        define(f"A1{sign}{d}", term(y2, column(d), 0), lambda d=d: ra1.at[d], device)
+        define(f"A2p{d}", term(yp, column(d), 0), lambda d=d: ra2.at[0, d], to_yp)
+        define(f"A2m{d}", term(ym, column(d), 0), lambda d=d: ra2.at[1, d], to_ym)
+    for d, device in ((1, to_xp), (2, to_x2), (3, to_xm)):
+        define(f"A3{d}", term(y, column(d), 0), lambda d=d: ra3.at[d - 1], device)
     turns = (y2, yp, ym, y)
     for i in range(4):
         to_first = to_x2 if i == 3 else (to_xp if i % 2 == 0 else to_xm)
@@ -150,7 +153,7 @@
     for i, device in enumerate((to_y2, to_yp, to_ym)):
         define(f"B3{i}", term(turns[i], x, 288), lambda i=i: rb3.at[i], device)
 
-    for i in range(2):
+    for i in range(4):
         define(f"C0{i}", lambda i=i: up.at[i, f1], lambda i=i: uc.at[i, 0], to_core)
         define(f"C1{i}", lambda i=i: up.at[i, f3], lambda i=i: uc.at[i, 1], to_core)
         for j, device in enumerate((to_pair, to_far, to_z2)):
@@ -160,17 +163,23 @@
         for j, device in enumerate((to_xp, to_xm, to_x2)):
             define(f"X{j}{i}", lambda i=i: us3.at[i], lambda i=i, j=j: uxr.at[i, j], device)
 
-    kbuf[y * 4 + x] = lat[...]
     barrier = pltpu.get_barrier_semaphore()
     partners = (to_xp, to_xm, to_x2, to_yp, to_ym, to_y2, to_pair, to_core, to_far, to_z2)
     for partner in partners:
         pl.semaphore_signal(barrier, inc=1, device_id=partner, device_id_type=MESH)
-    pl.semaphore_wait(barrier, len(partners))
-
-    start("wk2", "qn", "a1", "b1", "a2", "b2", "a5", "b5", "a3", "b3", "a4", "b4", "qr", "wk1")
-    w_all[f] = w_own[...]
+    pairs = ((w_in, w_own), (nope_in, nope_o), (lat_in, lat), (rope_in, rope_o), (gout_in, gout_o))
+    copies = [pltpu.make_async_copy(source, target, loads.at[i]) for i, (source, target) in enumerate(pairs)]
+    for copy in copies:
+        copy.start()
     query[:, 512:640, :] = jnp.zeros((4, 128, 512), BF16)
     keys[:, :, 512:640] = jnp.zeros((8, 256, 128), BF16)
+    for copy in copies:
+        copy.wait()
+    kbuf[y * 4 + x] = lat[...]
+    w_all[f] = w_own[...]
+    pl.semaphore_wait(barrier, len(partners))
+
+    start("wk2", "qn", "a1", "b1", "a2", "b2", "a5", "b5", "a3", "b3", "a4", "b4", "qr", "wk1")
 
     def place_rope(rope, s):
         for k in range(4):
@@ -227,6 +236,8 @@
         lax.fori_loop(0, 4, two_heads, 0)
 
     wait("wk1", "wk3")
+    wait("wv2")
+    start("wv3")
     project(nope_o, 0, query, 0)
     for s in range(4):
         wk_t[:, s * 128 : s * 128 + 128] = jnp.transpose(w_all[s, :, 0:1024])
@@ -234,33 +245,34 @@
     place_rope(rope_p, 1)
     project(nope_p, 0, query, 1)
 
-    for name in ("a", "b"):
-        wait(*(name + n for n in ("4", "8", "9", "11", "13", "14", "15", "16")))
-
-    def assemble(i, _):
-        yy, xx = i // 2, (i % 2) * 2
+    def assemble(yy, xx):
         both = [kbuf[yy * 4 + xx + j] for j in range(2)]
-        lanes = pl.ds(pl.multiple_of(i * 128, 128), 128)
-        high_lanes = pl.ds(pl.multiple_of(1024 + i * 128, 128), 128)
+        lanes = pl.ds(pl.multiple_of(yy * 256 + xx * 64, 128), 128)
+        high_lanes = pl.ds(pl.multiple_of(1024 + yy * 256 + xx * 64, 128), 128)
         keys_t[:, lanes] = jnp.concatenate([b[:, :64] for b in both], axis=1)
         keys_t[:, high_lanes] = jnp.concatenate([b[:, 64:] for b in both], axis=1)
         for j in range(2):
-            rows = pl.ds(pl.multiple_of((xx + j) * 64, 64), 64)
+            rows = slice((xx + j) * 64, (xx + j) * 64 + 64)
             main = jnp.transpose(both[j][:512])
             rest = jnp.transpose(both[j][512:])
             keys[yy, rows, 0:512] = main[:64]
             keys[yy, rows, 512:576] = rest[:64]
             keys[4 + yy, rows, 0:512] = main[64:]
             keys[4 + yy, rows, 512:576] = rest[64:]
-        return 0
-
-    lax.fori_loop(0, 8, assemble, 0)
-    wait("wv2")
-    start("wv3")
+
+    def key_row(yy, *names):
+        wait(*names)
+        assemble(yy, 0)
+        assemble(yy, 2)
+
+    key_row(y, "b4", "b13")
+    key_row(yp, "a4", "a8", "b9", "b15")
+    key_row(ym, "a9", "a11", "b8", "b14")
     wait("wv1", "wv3")
     project(gout_o, 1024, grad, 0)
-
-    peak[...] = jnp.full((4, 1, 512), NEG_FILL, F32)
+    key_row(y2, "a13", "a14", "a15", "a16", "b11", "b16")
+
+    peak[...] = jnp.full((4, 1, 512), NEG_START, F32)
     total[...] = jnp.zeros((4, 1, 512), F32)
     centre[...] = jnp.zeros((4, 1, 512), F32)
     relative = lax.broadcasted_iota(jnp.int32, (64, 512), 0) - lax.broadcasted_iota(jnp.int32, (64, 512), 1) % 64
@@ -277,14 +289,11 @@
                 key_first = order[0, (t * 2 + zl) * 4 + xx]
                 key_block = 63 - key_first if high else key_first
                 parts.append(relative <= (block - key_block) * 64)
-            allowed = jnp.concatenate(parts, axis=0)
-            scores = jnp.where(allowed, scores, NEG_FILL)
+            scores = jnp.where(jnp.concatenate(parts, axis=0), scores, NEG_FILL)
         old = peak[g]
         new = jnp.maximum(old, jnp.max(scores, axis=0, keepdims=True))
-        weights = jnp.exp((scores - new) * SCALE)
-        if masked:
-            weights = jnp.where(allowed, weights, 0.0)
-        factor = jnp.exp((old - new) * SCALE)
+        weights = jnp.exp2((scores - new) * BASE2)
+        factor = jnp.exp2((old - new) * BASE2)
         total[g] = total[g] * factor + jnp.sum(weights, axis=0, keepdims=True)
         centre[g] = centre[g] * factor + jnp.sum(weights * grad_probs, axis=0, keepdims=True)
         peak[g] = new
@@ -312,24 +321,18 @@
     visits(1, order[0, pair_blk])
 
     def normalise(slot, g):
-        factor = jnp.exp((peaks[slot] - peak[g]) * SCALE) / total[g]
+        factor = jnp.exp2((peaks[slot] - peak[g]) * BASE2) / total[g]
         p = probs[slot].astype(F32) * factor
         probs[slot] = p.astype(BF16)
         gscore[slot] = (p * (gprob[slot] - centre[g]) * SCALE).astype(BF16)
-
-    def low_rows(ref, g):
-        return ref[g * 4 : g * 4 + 4].reshape(1024, 512)
-
-    def all_rows(ref, g):
-        return jnp.concatenate([low_rows(ref, g), ref[16 + g * 2 : 20 + g * 2].reshape(1024, 512)], axis=0)
 
     def merge(s):
         wait(f"st{1 - s}")
         for g in (2 * s, 2 * s + 1):
             here, there = stat_s[g], stat_r[g]
             new = jnp.maximum(here[0:1], there[0:1])
-            f_here = jnp.exp((here[0:1] - new) * SCALE)
-            f_there = jnp.exp((there[0:1] - new) * SCALE)
+            f_here = jnp.exp2((here[0:1] - new) * BASE2)
+            f_there = jnp.exp2((there[0:1] - new) * BASE2)
             norm = here[1:2] * f_here + there[1:2] * f_there
             peak[g] = new
             total[g] = norm
@@ -345,33 +348,26 @@
 
         lax.fori_loop(0, 8, low_slots, 0)
         lax.fori_loop(0, 4, high_slots, 0)
-        out_t[2 * s] = mm(keys_t[0:512, :], all_rows(probs, 2 * s)).astype(BF16)
-        out_t[2 * s + 1] = mm(keys_t[0:512, 0:1024], low_rows(probs, 2 * s + 1)).astype(BF16)
-
-    merge(1)
-    merge(0)
-
-    def two_heads_of(ref, k):
-        lanes = pl.ds(pl.multiple_of(k * 128, 128), 128)
-        return jnp.concatenate([ref[g, 0:512, lanes] for g in range(4)], axis=1)
+
+    def times_keys(ref, rows, source, s, lanes):
+        low = source[8 * s : 8 * s + 4, :, lanes].reshape(1024, -1)
+        high = source[16 + 4 * s : 20 + 4 * s, :, lanes].reshape(1024, -1)
+        ref[2 * s, :, lanes] = mm(keys_t[rows, :], jnp.concatenate([low, high], axis=0)).astype(BF16)
+        low = source[8 * s + 4 : 8 * s + 8, :, lanes].reshape(1024, -1)
+        ref[2 * s + 1, :, lanes] = mm(keys_t[rows, 0:1024], low).astype(BF16)
 
     def two_heads_rows(own, pair, k):
-        lanes = pl.ds(pl.multiple_of(k * 256, 256), 256)
+        lanes = slice(k * 256, k * 256 + 256)
         mine, other = blocks(own, lanes), blocks(pair, lanes)
         return jnp.concatenate([mine[128:], mine[:128], other[128:], other[:128]], axis=0)
 
-    def value_terms(k, _):
-        lanes = pl.ds(pl.multiple_of(k * 256, 256), 256)
-        whole = mm(two_heads_of(out_t, k), two_heads_rows(gout_o, gout_p, k))
-        up[0, :, :, lanes] = whole.astype(BF16).reshape(4, 128, 256)
-        return 0
-
-    lax.fori_loop(0, 4, value_terms, 0)
-    start("C00", "C10")
-
-    for s in (1, 0):
-        dq_t[2 * s] = mm(keys_t[...], all_rows(gscore, 2 * s)).astype(BF16)
-        dq_t[2 * s + 1] = mm(keys_t[:, 0:1024], low_rows(gscore, 2 * s + 1)).astype(BF16)
+    def weight_terms(i, ref, own, pair):
+        for j in range(2):
+            k = (i % 2) * 2 + j
+            left = jnp.concatenate([ref[g, 0:512, k * 128 : k * 128 + 128] for g in range(4)], axis=1)
+            whole = mm(left, two_heads_rows(own, pair, k))
+            up[i, :, :, j * 256 : j * 256 + 256] = whole.astype(BF16).reshape(4, 128, 256)
+        start(f"C0{i}", f"C1{i}")
 
     def sum_core(i):
         wait(f"C0{i}", f"C1{i}")
@@ -381,24 +377,6 @@
                 whole = up[i, shard, rows].astype(F32) + uc[i, slot, rows].astype(F32)
                 uzs[i, j, yy] = whole.astype(BF16)
         start(f"Z0{i}", f"Z1{i}", f"Z2{i}")
-
-    sum_core(0)
-
-    def key_terms(k, _):
-        lanes = pl.ds(pl.multiple_of(k * 256, 256), 256)
-        left = two_heads_of(dq_t, k)
-        whole = mm(left, two_heads_rows(nope_o, nope_p, k))
-        up[1, :, :, lanes] = whole.astype(BF16).reshape(4, 128, 256)
-        back = mm(wk_t[lanes, :], left)
-        for j in range(2):
-            rows = pl.ds(pl.multiple_of(k * 256 + j * 128, 128), 128)
-            tiles = [back[j * 128 : j * 128 + 128, g * 128 + j * 64 : g * 128 + j * 64 + 64] for g in range(4)]
-            gn_own[rows, :] = jnp.concatenate([tiles[1], tiles[0]], axis=1)
-            gn_send[rows, :] = jnp.concatenate([tiles[3], tiles[2]], axis=1).astype(BF16)
-        return 0
-
-    lax.fori_loop(0, 4, key_terms, 0)
-    start("C01", "C11")
 
     def sum_z(i):
         wait(f"Z0{i}", f"Z1{i}", f"Z2{i}")
@@ -416,29 +394,32 @@
         us3[i] = whole.astype(BF16)
         start(f"X0{i}", f"X1{i}", f"X2{i}")
 
-    def sum_x(i, lanes):
+    def sum_x(i):
         wait(f"X0{i}", f"X1{i}", f"X2{i}")
         whole = us3[i].astype(F32) + uxr[i, 0].astype(F32) + uxr[i, 1].astype(F32) + uxr[i, 2].astype(F32)
         mine_rows = whole[0:4]
         for xx in range(1, 4):
             mine_rows = jnp.where(x == xx, whole[xx * 4 : xx * 4 + 4], mine_rows)
-        gu_out[:, lanes] = mine_rows
-
-    lower = pl.ds(288, 288)
-
-    def b_second(i):
-        wait(f"B1{i}")
-        add_into(dkb.at[turns[i], xp if i % 2 == 0 else xm, lower], rb1.at[i])
-        start(f"B2p{i}", f"B2m{i}")
-
-    def b_last(i):
-        wait(f"B2p{i}", f"B2m{i}")
-        add_into(dkb.at[turns[i], x, lower], rb2.at[i, 0], rb2.at[i, 1])
-        start(f"B3{i}")
-
-    def key_turn(i, _):
-        t = (y + jnp.where(i == 0, 2, jnp.where(i == 1, 1, jnp.where(i == 2, 3, 0)))) % 4
-
+        first = (1024, 1536, 0, 512)[i]
+        gu_out[:, first : first + 512] = mine_rows
+
+    def back(s, ref):
+        def two_heads(k, _):
+            lanes = pl.ds(pl.multiple_of(k * 128, 128), 128)
+            rows = pl.ds(pl.multiple_of(k * 256, 256), 256)
+            left = jnp.concatenate([dq_t[2 * s + 1, 0:512, lanes], dq_t[2 * s, 0:512, lanes]], axis=1)
+            out = mm(wk_t[rows, :], left)
+            ref[pl.ds(pl.multiple_of(k * 256, 256), 128), :] = jnp.concatenate(
+                [out[:128, 0:64], out[:128, 128:192]], axis=1
+            ).astype(ref.dtype)
+            ref[pl.ds(pl.multiple_of(k * 256 + 128, 128), 128), :] = jnp.concatenate(
+                [out[128:, 64:128], out[128:, 192:256]], axis=1
+            ).astype(ref.dtype)
+            return 0
+
+        lax.fori_loop(0, 4, two_heads, 0)
+
+    def key_tile(t):
         def one(slots):
             a = sum(mm_nt(query[g, 0:576], gscore[slot]) for g, slot in slots)
             b = sum(mm_nt(grad[g], probs[slot]) for g, slot in slots)
@@ -451,46 +432,91 @@
             dkb[t, xx, 0:512] = jnp.concatenate([low[:, lanes], high[:, lanes]], axis=1).astype(BF16)
             dkb[t, xx, 512:576] = jnp.concatenate([low_rest[:, lanes], high_rest[:, lanes]], axis=1).astype(BF16)
 
-        @pl.when(i == 0)
-        def _():
-            start("A1p", "A1m", "B10")
-            sum_core(1)
-            start("ro0", "ro1", "gn")
+    upper, lower = pl.ds(0, 288), pl.ds(288, 288)
+
+    def b_second(i):
+        wait(f"B1{i}")
+        add_into(dkb.at[turns[i], xp if i % 2 == 0 else xm, lower], rb1.at[i])
+        start(f"B2p{i}", f"B2m{i}")
+
+    def b_last(i):
+        wait(f"B2p{i}", f"B2m{i}")
+        add_into(dkb.at[turns[i], x, lower], rb2.at[i, 0], rb2.at[i, 1])
+        start(f"B3{i}")
+
+    every, halves = slice(0, 512), (slice(0, 256), slice(256, 512))
+    main, full = slice(0, 512), slice(0, 576)
+    merge(1)
+    times_keys(out_t, main, probs, 1, every)
+    merge(0)
+    times_keys(out_t, main, probs, 0, halves[0])
+    weight_terms(0, out_t, gout_o, gout_p)
+    times_keys(out_t, main, probs, 0, halves[1])
+    weight_terms(1, out_t, gout_o, gout_p)
+    key_tile(y2)
+    start("A1p2", "A1m3", "A1p1", "A1m0", "B10")
+    sum_core(0)
+    sum_core(1)
+    times_keys(dq_t, full, gscore, 1, every)
+    back(1, gn_send)
+    start("ro0", "ro1", "gn")
+    times_keys(dq_t, full, gscore, 0, halves[0])
+    weight_terms(2, dq_t, nope_o, nope_p)
+    b_second(0)
+    times_keys(dq_t, full, gscore, 0, halves[1])
+    weight_terms(3, dq_t, nope_o, nope_p)
+    sum_core(2)
+    sum_z(0)
+
+    def key_turn(i, _):
+        key_tile((y + jnp.where(i == 1, 1, jnp.where(i == 2, 3, 0))) % 4)
 
         @pl.when(i == 1)
         def _():
-            start("B11")
-            wait("A1p")
-            add_into(dkb.at[yp, pl.ds(0, 2), pl.ds(0, 288)], ra1.at[0])
-            start("A2p")
-            b_second(0)
+            for d in (2, 1):
+                wait(f"A1p{d}")
+                add_into(dkb.at[yp, column(d), upper], ra1.at[d])
+                start(f"A2p{d}")
+            start("B11", "A2p3", "A2p0")
+            sum_core(3)
+            b_last(0)
+            sum_z(1)
 
         @pl.when(i == 2)
         def _():
-            start("B12")
-            wait("A1m")
-            add_into(dkb.at[ym, pl.ds(2, 2), pl.ds(0, 288)], ra1.at[1])
-            start("A2m")
+            start("A2m2", "A2m1", "B12")
+            for d in (3, 0):
+                wait(f"A1m{d}")
+                add_into(dkb.at[ym, column(d), upper], ra1.at[d])
+                start(f"A2m{d}")
             b_second(1)
-            b_last(0)
-            sum_z(0)
+            sum_y(0)
 
         @pl.when(i == 3)
         def _():
             start("B13", "B2p3", "B2m3")
-            wait("A2p", "A2m")
-            add_into(dkb.at[y, :, pl.ds(0, 288)], ra2.at[0], ra2.at[1])
-            start("A3p", "A3m", "A32")
             b_second(2)
             b_last(1)
-            sum_z(1)
-            sum_y(0)
+            sum_y(1)
+            sum_z(2)
 
         return 0
 
-    lax.fori_loop(0, 4, key_turn, 0)
+    lax.fori_loop(1, 4, key_turn, 0)
+    def a_last(d):
+        wait(f"A2p{d}", f"A2m{d}")
+        add_into(dkb.at[y, column(d), upper], ra2.at[0, d], ra2.at[1, d])
+        start(f"A3{d}")
+
+    a_last(2)
+    back(0, gn_own)
+    a_last(1)
+    a_last(3)
+    sum_z(3)
     b_last(2)
-    sum_y(1)
+    sum_x(0)
+    sum_x(1)
+    sum_y(2)
 
     wait("gn", "ro0", "ro1")
     gn_out[...] = jnp.transpose(gn_own[...] + gn_recv[...].astype(F32)).astype(BF16)
@@ -500,15 +526,21 @@
             [rope[h * 64 : h * 64 + 64] for h in range(HEADS)], axis=1
         ).astype(BF16)
 
-    wait("A3p", "A3m", "A32")
-    add_into(dkb.at[y, x, pl.ds(0, 288)], ra3.at[0], ra3.at[1], ra3.at[2])
+    sum_y(3)
+    wait("A31", "A32", "A33", "A2p0", "A2m0")
+    add_into(dkb.at[y, x, upper], ra2.at[0, 0], ra2.at[1, 0], ra3.at[0], ra3.at[1], ra3.at[2])
     wait("B13", "B2p3", "B2m3", "B30", "B31", "B32")
     add_into(dkb.at[y, x, lower], rb1.at[3], rb2.at[3, 0], rb2.at[3, 1], rb3.at[0], rb3.at[1], rb3.at[2])
     gl_out[...] = dkb[y, x]
-    sum_x(0, slice(1024, 2048))
-    sum_x(1, slice(0, 1024))
+    sum_x(2)
+    sum_x(3)
     for name in made:
         made[name]().wait_send()
+
+
+def hand_over(*refs):
+    for source, target in zip(refs[:4], refs[4:]):
+        target[...] = source[...]
 
 
 def per_device(query_nope, query_rope, latent, grad_out, w_up, block_order):
@@ -518,10 +550,11 @@
         ((4, 640, 512), BF16), ((4, 512, 512), BF16), ((24, 256, 512), BF16), ((24, 256, 512), F32), ((24, 256, 512), BF16),
         ((24, 1, 512), F32), ((4, 1, 512), F32), ((4, 1, 512), F32), ((4, 1, 512), F32), ((4, 8, 512), F32), ((4, 8, 512), F32),
         ((4, 576, 512), BF16), ((4, 512, 512), BF16), ((1024, 128), F32), ((1024, 128), BF16), ((1024, 128), BF16), ((2, 64, 512), BF16),
-        ((4, 4, 576, 128), BF16), ((2, 2, 288, 128), BF16), ((2, 4, 288, 128), BF16), ((3, 288, 128), BF16),
+        ((4, 4, 576, 128), BF16), ((4, 288, 128), BF16), ((2, 4, 288, 128), BF16), ((3, 288, 128), BF16),
         ((4, 288, 128), BF16), ((4, 2, 288, 128), BF16), ((3, 288, 128), BF16),
-        ((2, 4, 128, 1024), BF16), ((2, 2, 128, 1024), BF16), ((2, 3, 4, 16, 1024), BF16), ((2, 3, 4, 16, 1024), BF16),
-        ((2, 4, 16, 1024), BF16), ((2, 3, 16, 1024), BF16), ((2, 16, 1024), BF16), ((2, 3, 16, 1024), BF16),
+        ((4, 4, 128, 512), BF16), ((4, 2, 128, 512), BF16), ((4, 3, 4, 16, 512), BF16), ((4, 3, 4, 16, 512), BF16),
+        ((4, 4, 16, 512), BF16), ((4, 3, 16, 512), BF16), ((4, 16, 512), BF16), ((4, 3, 16, 512), BF16),
+        ((576, 128), BF16), ((128, 1024), BF16), ((128, 512), BF16), ((128, 1024), BF16), ((128, 2048), BF16),
     ]
     vmem = pl.BlockSpec(memory_space=pltpu.VMEM)
     gn, gr, gl, gu = pl.pallas_call(
@@ -532,15 +565,22 @@
             jax.ShapeDtypeStruct((576, 128), BF16),
             jax.ShapeDtypeStruct((4, 2048), F32),
         ),
-        in_specs=[pl.BlockSpec(memory_space=pltpu.SMEM)] + [vmem] * 5,
+        in_specs=[pl.BlockSpec(memory_space=pltpu.SMEM)] + [pl.BlockSpec(memory_space=pl.ANY)] * 5,
         out_specs=(vmem,) * 4,
         scratch_shapes=[pltpu.VMEM(shape, dtype) for shape, dtype in shapes]
-        + [pltpu.SemaphoreType.DMA((COPIES,)), pltpu.SemaphoreType.DMA((COPIES,))],
+        + [pltpu.SemaphoreType.DMA((5,)), pltpu.SemaphoreType.DMA((COPIES,)), pltpu.SemaphoreType.DMA((COPIES,))],
         compiler_params=pltpu.CompilerParams(
             collective_id=0, has_side_effects=True, vmem_limit_bytes=63 * 1024 * 1024
         ),
         name="latent_attention_backward",
     )(block_order.T, latent[0].T, query_nope[0], query_rope[0], grad_out[0], w_up)
+    gn, gr, gl, gu = pl.pallas_call(
+        hand_over,
+        out_shape=tuple(jax.ShapeDtypeStruct(a.shape, a.dtype) for a in (gn, gr, gl, gu)),
+        in_specs=[vmem] * 4,
+        out_specs=(vmem,) * 4,
+        name="hand_over",
+    )(gn, gr, gl, gu)
     return gn[None], gr[None], gl.T[None], gu
 
 

time: 92.3 us -> 85.5 us (0.926)
  local copies, waits for them, and re-layouts: 4.04 us -> 0 us
  Pallas kernels: 86.7 us -> 84.7 us
    unnamed x10 -> x0, local copies, waits for them, and re-layouts: 4.04 us -> none
    pallas_call x1, Pallas kernels: 86.7 us -> 82.8 us  [per_device(): pl.pallas_call(kernel, out_shape=(jax.ShapeDtypeStruct((128, 1024), BF16)...]
    pallas_call x0 -> x1, Pallas kernels: none -> 1.86 us  [per_device(): pl.pallas_call(hand_over, out_shape=tuple((jax.ShapeDtypeStruct(a.shape,...]
where the time goes in v3:
time: 85.5 us; the launch traced here: 85.3 us
  Pallas kernels  84.7 us (99%)
    pallas_call x1, Pallas kernels, per_device(): pl.pallas_call(kernel, out_shape=(jax.ShapeDtypeStruct((128, 1024), BF16)...  82.8 us
    pallas_call x1, Pallas kernels, per_device(): pl.pallas_call(hand_over, out_shape=tuple((jax.ShapeDtypeStruct(a.shape,...  1.86 us

profile of v3, /device:TPU:0, one launch (start us, length us, event | category | flops | bytes accessed | tf_op | source)
XLA Modules:
  0.0 85.3 jit_solution(11705065504162446853)
XLA Ops:
  0.6 82.8 %latent_attention_backward.1 = (bf16[128,1024]{1,0:T(8,128)(2,1)}, bf16[128,512]{1,0:T(8,128)(2,1)}, bf16[576,128]{1,0:T(8,128)(2,1)}, f32[4,2048]{1,0:T(4,128)}) custom-call(s32[2,32]{1,0:T(2,128)} %bitcast.16, bf16[576,128]{1,0:T(8,128)(2,1)} %bitcast.14, bf16[128,1024]{1,0:T(8,128)(2,1)} %bitcast.12, bf16[128,512]{1,0:T(8,128)(2,1)} %bitcast.15, ...), custom_call_target="tpu_custom_call" | custom-call | tf_op jit(solution)/shard_map/latent_attention_backward/pallas_call | solution.py:560
  83.4 1.9 %hand_over.1 = (bf16[128,1024]{1,0:T(8,128)(2,1)}, bf16[128,512]{1,0:T(8,128)(2,1)}, bf16[576,128]{1,0:T(8,128)(2,1)}, f32[4,2048]{1,0:T(4,128)}) custom-call(bf16[128,1024]{1,0:T(8,128)(2,1)} %get-tuple-element.12.refs_0_, bf16[128,512]{1,0:T(8,128)(2,1)} %get-tuple-element.13.refs_1_, bf16[576,128]{1,0:T(8,128)(2,1)} %get-tuple-element.14.refs_2_, ...), custom_call_target="tpu_custom_call" | custom-call | tf_op jit(solution)/shard_map/hand_over/pallas_call | solution.py:577

commit v4 on v3

--- a/solution.py
+++ b/solution.py
@@ -146,8 +146,7 @@
         define(f"A3{d}", term(y, column(d), 0), lambda d=d: ra3.at[d - 1], device)
     turns = (y2, yp, ym, y)
     for i in range(4):
-        to_first = to_x2 if i == 3 else (to_xp if i % 2 == 0 else to_xm)
-        define(f"B1{i}", term(turns[i], x2, 288), lambda i=i: rb1.at[i], to_first)
+        define(f"B1{i}", term(turns[i], x2, 288), lambda i=i: rb1.at[i], to_x2)
         define(f"B2p{i}", term(turns[i], xp, 288), lambda i=i: rb2.at[i, 0], to_xp)
         define(f"B2m{i}", term(turns[i], xm, 288), lambda i=i: rb2.at[i, 1], to_xm)
     for i, device in enumerate((to_y2, to_yp, to_ym)):
@@ -179,7 +178,7 @@
     w_all[f] = w_own[...]
     pl.semaphore_wait(barrier, len(partners))
 
-    start("wk2", "qn", "a1", "b1", "a2", "b2", "a5", "b5", "a3", "b3", "a4", "b4", "qr", "wk1")
+    start("wk2", "qn", "wv2", "a1", "b1", "a2", "b2", "a5", "b5", "a3", "b3", "a4", "b4", "qr", "wk1")
 
     def place_rope(rope, s):
         for k in range(4):
@@ -198,7 +197,7 @@
     for name in ("a", "b"):
         wait(name + "5")
         start(name + "11", name + "12")
-    start("wv2", "qg", "wv1")
+    start("qg", "wv1")
     for name in ("a", "b"):
         wait(name + "3")
         start(name + "13")
@@ -270,8 +269,6 @@
     key_row(ym, "a9", "a11", "b8", "b14")
     wait("wv1", "wv3")
     project(gout_o, 1024, grad, 0)
-    key_row(y2, "a13", "a14", "a15", "a16", "b11", "b16")
-
     peak[...] = jnp.full((4, 1, 512), NEG_START, F32)
     total[...] = jnp.zeros((4, 1, 512), F32)
     centre[...] = jnp.zeros((4, 1, 512), F32)
@@ -301,24 +298,31 @@
         gprob[slot] = grad_probs
         peaks[slot] = new
 
-    def visits(s, first):
-        def step(t, _):
+    def visits(s, first, begin, end):
+        def step(i, _):
+            t = (y + jnp.where(i == 0, 0, jnp.where(i == 1, 1, jnp.where(i == 2, 3, 2)))) % 4
             visit(t, 2 * s, False, False, first)
             visit(t, 2 * s + 1, False, True, first)
             visit(t, 2 * s, True, True, first)
             return 0
 
-        lax.fori_loop(0, 4, step, 0)
+        lax.fori_loop(begin, end, step, 0)
+
+    def tell(s):
         for g in (2 * s, 2 * s + 1):
             stat_s[g, 0:1] = peak[g]
             stat_s[g, 1:2] = total[g]
             stat_s[g, 2:3] = centre[g]
         start(f"st{s}")
 
-    visits(0, order[0, blk])
+    visits(0, order[0, blk], 0, 3)
+    key_row(y2, "a13", "a14", "a15", "a16", "b11", "b16")
+    visits(0, order[0, blk], 3, 4)
+    tell(0)
     wait("qg")
     project(gout_p, 1024, grad, 1)
-    visits(1, order[0, pair_blk])
+    visits(1, order[0, pair_blk], 0, 4)
+    tell(1)
 
     def normalise(slot, g):
         factor = jnp.exp2((peaks[slot] - peak[g]) * BASE2) / total[g]
@@ -434,89 +438,93 @@
 
     upper, lower = pl.ds(0, 288), pl.ds(288, 288)
 
-    def b_second(i):
-        wait(f"B1{i}")
-        add_into(dkb.at[turns[i], xp if i % 2 == 0 else xm, lower], rb1.at[i])
-        start(f"B2p{i}", f"B2m{i}")
+    def b_first(i):
+        start(f"B1{i}", f"B2p{i}", f"B2m{i}")
 
     def b_last(i):
-        wait(f"B2p{i}", f"B2m{i}")
-        add_into(dkb.at[turns[i], x, lower], rb2.at[i, 0], rb2.at[i, 1])
+        wait(f"B1{i}", f"B2p{i}", f"B2m{i}")
+        add_into(dkb.at[turns[i], x, lower], rb1.at[i], rb2.at[i, 0], rb2.at[i, 1])
         start(f"B3{i}")
 
     every, halves = slice(0, 512), (slice(0, 256), slice(256, 512))
     main, full = slice(0, 512), slice(0, 576)
+    def a_second(d, row, sign):
+        wait(f"A1{sign}{d}")
+        add_into(dkb.at[row, column(d), upper], ra1.at[d])
+        start(f"A2{sign}{d}")
+
     merge(1)
     times_keys(out_t, main, probs, 1, every)
     merge(0)
+
+    def first_turn(i, _):
+        key_tile((y + 2 - i) % 4)
+
+        @pl.when(i == 0)
+        def _():
+            start("A1p2", "A1m3", "A1p1", "A1m0")
+            b_first(0)
+
+        return 0
+
+    lax.fori_loop(0, 2, first_turn, 0)
+    start("A2p3", "A2p0")
+    b_first(1)
+    times_keys(dq_t, full, gscore, 1, every)
+    back(1, gn_send)
+    start("ro0", "ro1", "gn")
+    a_second(2, yp, "p")
+    a_second(1, yp, "p")
     times_keys(out_t, main, probs, 0, halves[0])
     weight_terms(0, out_t, gout_o, gout_p)
     times_keys(out_t, main, probs, 0, halves[1])
     weight_terms(1, out_t, gout_o, gout_p)
-    key_tile(y2)
-    start("A1p2", "A1m3", "A1p1", "A1m0", "B10")
     sum_core(0)
-    sum_core(1)
-    times_keys(dq_t, full, gscore, 1, every)
-    back(1, gn_send)
-    start("ro0", "ro1", "gn")
+    b_last(0)
     times_keys(dq_t, full, gscore, 0, halves[0])
     weight_terms(2, dq_t, nope_o, nope_p)
-    b_second(0)
+    sum_core(1)
     times_keys(dq_t, full, gscore, 0, halves[1])
     weight_terms(3, dq_t, nope_o, nope_p)
     sum_core(2)
-    sum_z(0)
+    b_last(1)
 
     def key_turn(i, _):
-        key_tile((y + jnp.where(i == 1, 1, jnp.where(i == 2, 3, 0))) % 4)
-
-        @pl.when(i == 1)
-        def _():
-            for d in (2, 1):
-                wait(f"A1p{d}")
-                add_into(dkb.at[yp, column(d), upper], ra1.at[d])
-                start(f"A2p{d}")
-            start("B11", "A2p3", "A2p0")
-            sum_core(3)
-            b_last(0)
-            sum_z(1)
+        key_tile((y + jnp.where(i == 2, 3, 0)) % 4)
 
         @pl.when(i == 2)
         def _():
-            start("A2m2", "A2m1", "B12")
-            for d in (3, 0):
-                wait(f"A1m{d}")
-                add_into(dkb.at[ym, column(d), upper], ra1.at[d])
-                start(f"A2m{d}")
-            b_second(1)
-            sum_y(0)
-
-        @pl.when(i == 3)
-        def _():
-            start("B13", "B2p3", "B2m3")
-            b_second(2)
-            b_last(1)
-            sum_y(1)
-            sum_z(2)
+            start("A2m2", "A2m1")
+            b_first(2)
+            sum_core(3)
+            a_second(3, ym, "m")
+            a_second(0, ym, "m")
+            sum_z(0)
+            sum_z(1)
 
         return 0
 
-    lax.fori_loop(1, 4, key_turn, 0)
+    lax.fori_loop(2, 4, key_turn, 0)
+    b_first(3)
+
     def a_last(d):
         wait(f"A2p{d}", f"A2m{d}")
         add_into(dkb.at[y, column(d), upper], ra2.at[0, d], ra2.at[1, d])
         start(f"A3{d}")
 
+    sum_z(2)
     a_last(2)
-    back(0, gn_own)
+    sum_z(3)
     a_last(1)
     a_last(3)
-    sum_z(3)
     b_last(2)
+    sum_y(0)
+    sum_y(1)
+    sum_y(2)
+    sum_y(3)
+    back(0, gn_own)
     sum_x(0)
     sum_x(1)
-    sum_y(2)
 
     wait("gn", "ro0", "ro1")
     gn_out[...] = jnp.transpose(gn_own[...] + gn_recv[...].astype(F32)).astype(BF16)
@@ -526,7 +534,6 @@
             [rope[h * 64 : h * 64 + 64] for h in range(HEADS)], axis=1
         ).astype(BF16)
 
-    sum_y(3)
     wait("A31", "A32", "A33", "A2p0", "A2m0")
     add_into(dkb.at[y, x, upper], ra2.at[0, 0], ra2.at[1, 0], ra3.at[0], ra3.at[1], ra3.at[2])
     wait("B13", "B2p3", "B2m3", "B30", "B31", "B32")

time: 85.5 us -> 84.1 us (0.984)
  Pallas kernels: 84.7 us -> 83.3 us
    pallas_call x1, Pallas kernels: 82.8 us -> 81.5 us  [per_device(): pl.pallas_call(kernel, out_shape=(jax.ShapeDtypeStruct((128, 1024), BF16)...]
where the time goes in v4:
time: 84.1 us; the launch traced here: 84 us
  Pallas kernels  83.3 us (99%)
    pallas_call x1, Pallas kernels, per_device(): pl.pallas_call(kernel, out_shape=(jax.ShapeDtypeStruct((128, 1024), BF16)...  81.5 us
    pallas_call x1, Pallas kernels, per_device(): pl.pallas_call(hand_over, out_shape=tuple((jax.ShapeDtypeStruct(a.shape,...  1.86 us

profile of v4, /device:TPU:0, one launch (start us, length us, event | category | flops | bytes accessed | tf_op | source)
XLA Modules:
  0.0 84.0 jit_solution(6603729881169625477)
XLA Ops:
  0.6 81.5 %latent_attention_backward.1 = (bf16[128,1024]{1,0:T(8,128)(2,1)}, bf16[128,512]{1,0:T(8,128)(2,1)}, bf16[576,128]{1,0:T(8,128)(2,1)}, f32[4,2048]{1,0:T(4,128)}) custom-call(s32[2,32]{1,0:T(2,128)} %bitcast.16, bf16[576,128]{1,0:T(8,128)(2,1)} %bitcast.14, bf16[128,1024]{1,0:T(8,128)(2,1)} %bitcast.12, bf16[128,512]{1,0:T(8,128)(2,1)} %bitcast.15, ...), custom_call_target="tpu_custom_call" | custom-call | tf_op jit(solution)/shard_map/latent_attention_backward/pallas_call | solution.py:567
  82.1 1.9 %hand_over.1 = (bf16[128,1024]{1,0:T(8,128)(2,1)}, bf16[128,512]{1,0:T(8,128)(2,1)}, bf16[576,128]{1,0:T(8,128)(2,1)}, f32[4,2048]{1,0:T(4,128)}) custom-call(bf16[128,1024]{1,0:T(8,128)(2,1)} %get-tuple-element.12.refs_0_, bf16[128,512]{1,0:T(8,128)(2,1)} %get-tuple-element.13.refs_1_, bf16[576,128]{1,0:T(8,128)(2,1)} %get-tuple-element.14.refs_2_, ...), custom_call_target="tpu_custom_call" | custom-call | tf_op jit(solution)/shard_map/hand_over/pallas_call | solution.py:584

commit v5 on v4

--- a/solution.py
+++ b/solution.py
@@ -37,13 +37,13 @@
 
 def kernel(
     order, lat_in, nope_in, rope_in, gout_in, w_in,
-    gn_out, gr_out, gl_out, gu_out,
+    gn_far, gr_far, gl_far, gu_far,
     kbuf, keys, keys_t, nope_p, rope_p, gout_p, w_all, wk_t,
     query, grad, probs, gprob, gscore, peaks, peak, total, centre, stat_s, stat_r,
     dq_t, out_t, gn_own, gn_send, gn_recv, ro_recv,
     dkb, ra1, ra2, ra3, rb1, rb2, rb3,
     up, uc, uzs, uz, us2, uyr, us3, uxr,
-    lat, nope_o, rope_o, gout_o, w_own, loads,
+    lat, nope_o, rope_o, gout_o, w_own, loads, gn_out, gr_out, gl_out, gu_out, stores,
     send, recv,
 ):
     f = lax.axis_index("fsdp")
@@ -534,15 +534,23 @@
             [rope[h * 64 : h * 64 + 64] for h in range(HEADS)], axis=1
         ).astype(BF16)
 
+    pairs = ((gn_out, gn_far), (gr_out, gr_far), (gl_out, gl_far), (gu_out, gu_far))
+    leave = [pltpu.make_async_copy(source, target, stores.at[i]) for i, (source, target) in enumerate(pairs)]
+    leave[0].start()
+    leave[1].start()
     wait("A31", "A32", "A33", "A2p0", "A2m0")
     add_into(dkb.at[y, x, upper], ra2.at[0, 0], ra2.at[1, 0], ra3.at[0], ra3.at[1], ra3.at[2])
     wait("B13", "B2p3", "B2m3", "B30", "B31", "B32")
     add_into(dkb.at[y, x, lower], rb1.at[3], rb2.at[3, 0], rb2.at[3, 1], rb3.at[0], rb3.at[1], rb3.at[2])
     gl_out[...] = dkb[y, x]
+    leave[2].start()
     sum_x(2)
     sum_x(3)
+    leave[3].start()
     for name in made:
         made[name]().wait_send()
+    for copy in leave:
+        copy.wait()
 
 
 def hand_over(*refs):
@@ -573,9 +581,11 @@
             jax.ShapeDtypeStruct((4, 2048), F32),
         ),
         in_specs=[pl.BlockSpec(memory_space=pltpu.SMEM)] + [pl.BlockSpec(memory_space=pl.ANY)] * 5,
-        out_specs=(vmem,) * 4,
+        out_specs=(pl.BlockSpec(memory_space=pl.ANY),) * 4,
         scratch_shapes=[pltpu.VMEM(shape, dtype) for shape, dtype in shapes]
-        + [pltpu.SemaphoreType.DMA((5,)), pltpu.SemaphoreType.DMA((COPIES,)), pltpu.SemaphoreType.DMA((COPIES,))],
+        + [pltpu.SemaphoreType.DMA((5,))]
+        + [pltpu.VMEM((128, 1024), BF16), pltpu.VMEM((128, 512), BF16), pltpu.VMEM((576, 128), BF16), pltpu.VMEM((4, 2048), F32)]
+        + [pltpu.SemaphoreType.DMA((4,)), pltpu.SemaphoreType.DMA((COPIES,)), pltpu.SemaphoreType.DMA((COPIES,))],
         compiler_params=pltpu.CompilerParams(
             collective_id=0, has_side_effects=True, vmem_limit_bytes=63 * 1024 * 1024
         ),

time: 84.1 us -> 83.8 us (level)
  no operation moved by 1% of the time
where the time goes in v5:
time: 83.8 us; the launch traced here: 83.6 us
  Pallas kernels  83 us (99%)
    pallas_call x1, Pallas kernels, per_device(): pl.pallas_call(kernel, out_shape=(jax.ShapeDtypeStruct((128, 1024), BF16)...  81.1 us
    pallas_call x1, Pallas kernels, per_device(): pl.pallas_call(hand_over, out_shape=tuple((jax.ShapeDtypeStruct(a.shape,...  1.86 us

profile of v5, /device:TPU:0, one launch (start us, length us, event | category | flops | bytes accessed | tf_op | source)
XLA Modules:
  0.0 83.6 jit_solution(268778452734257647)
XLA Ops:
  0.6 81.1 %latent_attention_backward.1 = (bf16[128,1024]{1,0:T(8,128)(2,1)}, bf16[128,512]{1,0:T(8,128)(2,1)}, bf16[576,128]{1,0:T(8,128)(2,1)}, f32[4,2048]{1,0:T(4,128)}) custom-call(s32[2,32]{1,0:T(2,128)} %bitcast.16, bf16[576,128]{1,0:T(8,128)(2,1)} %bitcast.14, bf16[128,1024]{1,0:T(8,128)(2,1)} %bitcast.12, bf16[128,512]{1,0:T(8,128)(2,1)} %bitcast.15, ...), custom_call_target="tpu_custom_call" | custom-call | tf_op jit(solution)/shard_map/latent_attention_backward/pallas_call | solution.py:575
  81.7 1.9 %hand_over.1 = (bf16[128,1024]{1,0:T(8,128)(2,1)}, bf16[128,512]{1,0:T(8,128)(2,1)}, bf16[576,128]{1,0:T(8,128)(2,1)}, f32[4,2048]{1,0:T(4,128)}) custom-call(bf16[128,1024]{1,0:T(8,128)(2,1)} %get-tuple-element.12.refs_0_, bf16[128,512]{1,0:T(8,128)(2,1)} %get-tuple-element.13.refs_1_, bf16[576,128]{1,0:T(8,128)(2,1)} %get-tuple-element.14.refs_2_, ...), custom_call_target="tpu_custom_call" | custom-call | tf_op jit(solution)/shard_map/hand_over/pallas_call | solution.py:594
